TPU v7x, 256 devices: a whole 4x4x8 slice. The times are simulated.
256 devices in a mesh: row: 16 (over z, x_lo), col: 16 (over y, x_hi, core).
Axes of the slice: x: 4 (x_hi: 2, x_lo: 2; x = x_hi * 2 + x_lo), y: 4, z: 8, core: 2. Of those that a mesh axis runs over, the one named last changes fastest.
Arguments:
- density: float32 [10240, 10240], P('row', 'col'), may hold values from -6 to 6
- core_hamiltonian: float32 [10240, 10240], P('row', 'col'), may hold values from -6 to 6
- class_tables: float32 [4, 256, 256], replicated, may hold values from -0.375 to 0.375
- shell_scale: float32 [10240], replicated, may hold values from 0.5 to 1.5
- block_place: int32 [640], replicated, may hold values from 0 to 639, as said below
- work_blocks: int32 [256, 32], P(('row', 'col')), may hold values from 0 to 639, as said below
- quartet_bra: int32 [256, 512], P(('row', 'col')), may hold values from 0 to 1023
- quartet_ket: int32 [256, 512], P(('row', 'col')), may hold values from 0 to 1023
- quartet_class: int32 [256, 512], P(('row', 'col')), may hold values from 0 to 3
- quartet_factor: float32 [256, 512], P(('row', 'col')), may hold values from 0.25 to 1
- quartet_count: int32 [256], P(('row', 'col')), may hold values from 1 to 512, 40960 in all
Outputs:
- fock_matrix: float32 [10240, 10240], P('row', 'col')
Inputs may be any that keep to these rules, and one draw needn't show every extreme that they name: `block_place`: a permutation of the 640 shell blocks. `work_blocks`: each device's 32 shell blocks are distinct and listed in increasing block_place; exactly 2 of them have places in each run of 40 = 40 consecutive places from 0 (one block row of devices), and likewise exactly 2 in each run of 40 = 40 (one block column of devices).
All inputs are finite; a program needn't handle non-finite values. No bound on the sum of `quartet_count` on one device may be relied on, other than what follows from the above.
Results may differ from a plain program's by a relative error of at most 0.0003.
Values sent between devices are 32-bit elements; how exact they have to be, the bound alone decides.
No kernel may reach another device: no remote copies, remote signals or barrier semaphores. Data moves between devices by JAX's collectives and lax.ppermute only.
A program may use at most 192 MiB of HBM per device.

v0:
```python
import jax
import jax.numpy as jnp
from jax import lax
from jax.sharding import PartitionSpec as P

SHELL = 16


ORDERS = (
    (3, 4, 0, 1, 2),
    (1, 2, 0, 3, 4),
    (2, 4, 0, 1, 3),
    (1, 3, 0, 2, 4),
    (2, 3, 0, 1, 4),
    (1, 4, 0, 2, 3),
)
COEFFS = (1.0, 1.0, -0.5, -0.5, -0.5, -0.5)


def make_class_stacks(class_tables):
    classes = class_tables.shape[0]
    pair_width = class_tables.shape[1]
    result = []
    for klass in range(classes):
        tensor = class_tables[klass].reshape(SHELL, SHELL, SHELL, SHELL)
        tables = []
        for layout in ORDERS:
            single = tuple((entry - 1 for entry in layout if entry != 0))
            tables.append(jnp.transpose(tensor, single).reshape(pair_width, pair_width))
        result.append(tables)
    return result


def pair_weights(weights):
    block_count = weights.shape[0]
    shell_width = weights.shape[1]
    outer = weights[:, None, :, None] * weights[None, :, None, :]
    return outer.reshape(block_count * block_count, shell_width * shell_width)


def class_terms(scaled, bra_pairs, ket_pairs, factors, tables, task_count):
    shell_a = bra_pairs // task_count
    shell_b = bra_pairs % task_count
    shell_c = ket_pairs // task_count
    shell_d = ket_pairs % task_count
    sources = (
        shell_c * task_count + shell_d,
        shell_a * task_count + shell_b,
        shell_b * task_count + shell_d,
        shell_a * task_count + shell_c,
        shell_b * task_count + shell_c,
        shell_a * task_count + shell_d,
    )
    targets = (sources[1], sources[0], sources[3], sources[2], sources[5], sources[4])
    values = []
    for source, table, weighting in zip(sources, tables, COEFFS):
        product = jnp.dot(scaled[source], table, precision=lax.Precision.HIGHEST)
        values.append(product * (weighting * factors)[:, None])
    return (jnp.concatenate(targets), jnp.concatenate(values))


def make_block_step(scaled, sorted_lists, tables, klass, block_rows, task_count):
    bra_pairs, ket_pairs, sorted_keys, factors = sorted_lists

    def block_step(block_index, running):
        offset = block_index * block_rows

        def window(values):
            return lax.dynamic_slice_in_dim(values, offset, block_rows, 0)

        keep = window(sorted_keys) == klass
        weighting = jnp.where(keep, window(factors), 0.0)
        targets, values = class_terms(
            scaled, window(bra_pairs), window(ket_pairs), weighting, tables, task_count
        )
        return running.at[targets].add(values)

    return block_step


def accumulate(totals, scaled, quartet_lists, begin_slot, end_slot, class_stacks, task_count):
    bra_pairs, ket_pairs, klasses, factors = quartet_lists
    slot_count = factors.shape[0]
    block_rows = min(slot_count, 128)
    classes = len(class_stacks)
    positions = jnp.arange(slot_count)
    inside = (positions >= begin_slot) & (positions < end_slot)
    sort_keys = jnp.where(inside, klasses, classes)
    order = jnp.argsort(sort_keys, stable=True)
    sorted_keys = sort_keys[order]
    sorted_lists = (
        bra_pairs[order],
        ket_pairs[order],
        sorted_keys,
        jnp.where(inside, factors, 0.0)[order],
    )
    class_counts = jnp.sum(
        (sorted_keys[None, :] == jnp.arange(classes)[:, None]).astype(jnp.int32), axis=1
    )
    class_ends = jnp.cumsum(class_counts)
    class_starts = class_ends - class_counts
    for klass in range(classes):
        step_fn = make_block_step(
            scaled, sorted_lists, class_stacks[klass], klass, block_rows, task_count
        )
        totals = lax.fori_loop(
            class_starts[klass] // block_rows,
            (class_ends[klass] + block_rows - 1) // block_rows,
            step_fn,
            totals,
        )
    return totals


def on_device(
    density,
    core_hamiltonian,
    class_tables,
    shell_scale,
    block_place,
    work_blocks,
    quartet_bra,
    quartet_ket,
    quartet_class,
    quartet_factor,
    quartet_count,
):
    row_count = lax.axis_size("row")
    col_count = lax.axis_size("col")
    task_count = work_blocks.shape[1]
    row_share = task_count // row_count
    col_share = task_count // col_count
    row_blocks = density.shape[0] // SHELL
    col_blocks = density.shape[1] // SHELL
    pair_width = SHELL * SHELL
    density_view = density.reshape(row_blocks, SHELL, col_blocks, SHELL)
    class_stacks = make_class_stacks(class_tables)
    scales = shell_scale.reshape(-1, SHELL)
    own_tasks = work_blocks[0]
    places = block_place[own_tasks]
    row_part = (places % row_blocks).reshape(row_count, row_share)
    col_part = (places % col_blocks).reshape(col_count, col_share)
    outgoing = jnp.concatenate(
        (
            jnp.broadcast_to(row_part[:, None, :], (row_count, col_count, row_share)),
            jnp.broadcast_to(col_part[None, :, :], (row_count, col_count, col_share)),
        ),
        axis=2,
    )
    incoming = lax.all_to_all(
        lax.all_to_all(outgoing, "row", split_axis=0, concat_axis=0, tiled=True),
        "col",
        split_axis=1,
        concat_axis=1,
        tiled=True,
    )
    wanted_rows = incoming[:, :, :row_share]
    wanted_cols = incoming[:, :, row_share:]
    row_index = jnp.transpose(wanted_rows, (0, 2, 1))[:, :, :, None]
    col_index = wanted_cols[:, None, :, :]
    layout = (row_count, row_share, col_count, col_share, pair_width)
    block_layout = (row_count, row_share, col_count, col_share, SHELL, SHELL)
    picked = density_view[row_index, :, col_index, :].reshape(layout)
    fetched = lax.all_to_all(
        lax.all_to_all(picked, "row", split_axis=0, concat_axis=0, tiled=True),
        "col",
        split_axis=2,
        concat_axis=2,
        tiled=True,
    )
    weights = pair_weights(scales[own_tasks])
    scaled = fetched.reshape(task_count * task_count, pair_width) * weights
    live_count = quartet_count[0]
    own_lists = (quartet_bra[0], quartet_ket[0], quartet_class[0], quartet_factor[0])
    zero_terms = jnp.zeros((task_count * task_count, pair_width), jnp.float32)
    fock_sums = jnp.zeros((row_blocks, SHELL, col_blocks, SHELL), jnp.float32)
    own_terms = accumulate(zero_terms, scaled, own_lists, 0, live_count, class_stacks, task_count)
    outbound = (own_terms * weights).reshape(layout)
    returned = lax.all_to_all(
        lax.all_to_all(outbound, "row", split_axis=0, concat_axis=0, tiled=True),
        "col",
        split_axis=2,
        concat_axis=2,
        tiled=True,
    )
    fock_sums = fock_sums.at[row_index, :, col_index, :].add(returned.reshape(block_layout))
    return core_hamiltonian + fock_sums.reshape(density.shape)


def solution(mesh):
    placed = (
        P("row", "col"),
        P("row", "col"),
        P(),
        P(),
        P(),
        P(("row", "col"), None),
        P(("row", "col"), None),
        P(("row", "col"), None),
        P(("row", "col"), None),
        P(("row", "col"), None),
        P(("row", "col")),
    )
    return jax.shard_map(
        on_device, mesh=mesh, in_specs=placed, out_specs=P("row", "col"), check_vma=False
    )
```

profile of v0, /device:TPU:1, one launch (start us, length us, event | category | flops | bytes accessed | tf_op | source)
XLA Modules:
  0.0 601.5 jit_solution(13936037272786962545)
XLA Ops:
  1.7 17.5 %all_to_all.30 = s32[16,16,4]{1,2,0:T(4,128)S(1)} all-to-all(s32[16,16,4]{1,2,0:T(4,128)S(1)} %copy.228), channel_id=1, replica_groups=mesh['row'=16,'col'=16] {'row'}, dimensions={0} | all-to-all | bytes 8192 | tf_op jit(solution)/shard_map/all_to_all | solution.py:151
  19.8 8.8 %all-to-all-start.1 = ((s32[16,16,4]{0,2,1:T(4,128)}), s32[16,16,4]{0,2,1:T(4,128)S(1)}, u32[]{:S(2)}, u32[]{:S(2)}) async-start(s32[16,16,4]{0,2,1:T(4,128)} %copy.229), calls=%async_computation.1 | async-start | bytes 65536 | tf_op jit(solution)/shard_map/all_to_all | solution.py:150
  28.6 8.5 %reshape.1347 = f32[40,16,40,16]{3,2,1,0:T(8,128)} reshape(f32[640,640]{1,0:T(8,128)} %param.19) | data formatting | bytes 3276800 | tf_op jit(solution)/shard_map/reshape | solution.py:136
  37.1 12.0 %copy.235 = f32[40,16,40,16]{3,1,2,0:T(8,128)} copy(f32[40,16,40,16]{3,2,1,0:T(8,128)} %reshape.1347) | data formatting | bytes 3276800 | tf_op jit(solution)/shard_map/reshape | solution.py:136
  50.9 16.1 %gather_fusion.28 = f32[1024,16,16]{2,1,0:T(8,128)} fusion(f32[40,16,40,16]{3,1,2,0:T(8,128)} %copy.235, s32[1024]{0:T(1024)S(1)} %reshape.1602), kind=kCustom, calls=%fused_computation.28 | custom fusion | bytes 2105344 | tf_op jit(solution)/shard_map/gather | solution.py:163
  67.0 7.4 %reshape.1348 = f32[16,2,16,2,256]{4,3,2,1,0:T(2,128)} reshape(f32[1024,16,16]{2,1,0:T(8,128)} %gather_fusion.28) | data formatting | bytes 2097152 | tf_op jit(solution)/shard_map/reshape | solution.py:163
  74.4 3.8 all-to-all-start.2
  78.8 3.8 sort.17
  82.6 3.5 gather_fusion.25
  86.5 18.7 %all-to-all-done.2 = f32[16,2,16,2,256]{4,3,2,1,0:T(2,128)S(1)} async-done(((f32[16,2,16,2,256]{4,3,2,1,0:T(2,128)}), f32[16,2,16,2,256]{4,3,2,1,0:T(2,128)S(1)}, u32[]{:S(2)}, u32[]{:S(2)}) %all-to-all-start.2) | async-done | bytes 1048608 | tf_op jit(solution)/shard_map/all_to_all | solution.py:165
  106.7 9.9 %all-to-all-start.3 = ((f32[16,2,16,2,256]{4,3,1,0,2:T(2,128)}), f32[16,2,16,2,256]{4,3,1,0,2:T(2,128)}, u32[]{:S(2)}, u32[]{:S(2)}) async-start(f32[16,2,16,2,256]{4,3,1,0,2:T(2,128)} %copy.236), calls=%async_computation.3 | async-start | bytes 2097152 | tf_op jit(solution)/shard_map/all_to_all | solution.py:164
  171.8 3.7 mul.478
  192.4 3.5 gather_fusion.30
  195.9 3.5 gather_fusion.26
  199.5 3.5 gather_fusion.27
  206.1 3.5 reshape.1358
  251.5 18.9 %while.52 = (s32[]{:T(128)}, f32[1024,256]{1,0:T(8,128)S(1)}, s32[]{:T(128)}, s32[512]{0:T(512)S(1)}, s32[512]{0:T(512)S(1)}, /*index=5*/f32[1024,256]{1,0:T(8,1...) while((s32[]{:T(128)}, f32[1024,256]{1,0:T(8,128)S(1)}, ...), condition=%wide.region_5.6_spmd, body=%wide.region_3.5_spmd.sunk | while | flops 604397568 | bytes 7142111 | solution.py:106
  264.0 6.5 %scatter_fusion = f32[1024,256]{1,0:T(8,128)S(1)} fusion(f32[1024,256]{1,0:T(8,128)S(1)} %get-tuple-element.1770, s32[768]{0:T(1024)S(1)} %fusion.183, f32[768,256]{1,0:T(8,128)S(1)} %fusion.189), kind=kCustom, calls=%fused_computation.31.clone.1 | custom fusion | flops 196608 | bytes 2362368 | tf_op jit(solution)/shard_map/while/body/scatter-add | solution.py:76
  270.4 19.3 %while.53 = (s32[]{:T(128)}, f32[1024,256]{1,0:T(8,128)S(1)}, s32[]{:T(128)}, s32[512]{0:T(512)S(1)}, s32[512]{0:T(512)S(1)}, /*index=5*/f32[1024,256]{1,0:T(8,1...) while((s32[]{:T(128)}, f32[1024,256]{1,0:T(8,128)S(1)}, ...), condition=%wide.region_8.9_spmd, body=%wide.region_6.8_spmd.sunk | while | flops 604397568 | bytes 7142111 | solution.py:106
  282.9 6.5 %scatter_fusion.1 = f32[1024,256]{1,0:T(8,128)S(1)} fusion(f32[1024,256]{1,0:T(8,128)S(1)} %get-tuple-element.1824, s32[768]{0:T(1024)S(1)} %fusion.202, f32[768,256]{1,0:T(8,128)S(1)} %fusion.208), kind=kCustom, calls=%fused_computation.32.clone.1 | custom fusion | flops 196608 | bytes 2362368 | tf_op jit(solution)/shard_map/while/body/scatter-add | solution.py:76
  289.7 18.9 %while.54 = (s32[]{:T(128)}, f32[1024,256]{1,0:T(8,128)S(1)}, s32[]{:T(128)}, s32[512]{0:T(512)S(1)}, s32[512]{0:T(512)S(1)}, /*index=5*/f32[1024,256]{1,0:T(8,1...) while((s32[]{:T(128)}, f32[1024,256]{1,0:T(8,128)S(1)}, ...), condition=%wide.region_11.12_spmd, body=%wide.region_9.11_spmd.sunk | while | flops 604397568 | bytes 7142111 | solution.py:106
  302.2 6.5 %scatter_fusion.2 = f32[1024,256]{1,0:T(8,128)S(1)} fusion(f32[1024,256]{1,0:T(8,128)S(1)} %get-tuple-element.1878, s32[768]{0:T(1024)S(1)} %fusion.221, f32[768,256]{1,0:T(8,128)S(1)} %fusion.227), kind=kCustom, calls=%fused_computation.33.clone.1 | custom fusion | flops 196608 | bytes 2362368 | tf_op jit(solution)/shard_map/while/body/scatter-add | solution.py:76
  308.6 18.1 %while.55 = (s32[]{:T(128)}, f32[1024,256]{1,0:T(8,128)S(1)}, s32[]{:T(128)}, s32[512]{0:T(512)S(1)}, s32[512]{0:T(512)S(1)}, /*index=5*/f32[1024,256]{1,0:T(8,1...) while((s32[]{:T(128)}, f32[1024,256]{1,0:T(8,128)S(1)}, ...), condition=%wide.region_14.15_spmd, body=%wide.region_12.14_spmd.sunk | while | flops 604397568 | bytes 7142111 | solution.py:106
  320.1 6.5 %scatter_fusion.3 = f32[1024,256]{1,0:T(8,128)S(1)} fusion(f32[1024,256]{1,0:T(8,128)S(1)} %get-tuple-element.1932, s32[768]{0:T(1024)S(1)} %fusion.240, f32[768,256]{1,0:T(8,128)S(1)} %fusion.246), kind=kCustom, calls=%fused_computation.34.clone.1 | custom fusion | flops 196608 | bytes 2362368 | tf_op jit(solution)/shard_map/while/body/scatter-add | solution.py:76
  329.1 86.3 %all_to_all.31 = f32[16,2,16,2,256]{4,3,2,1,0:T(2,128)S(1)} all-to-all(f32[16,2,16,2,256]{4,3,2,1,0:T(2,128)S(1)} %reshape.1371), channel_id=1, replica_groups=mesh['row'=16,'col'=16] {'row'}, dimensions={0} | all-to-all | bytes 2097152 | tf_op jit(solution)/shard_map/all_to_all | solution.py:180
  417.0 7.8 %all-to-all-start.5 = ((f32[16,2,16,2,256]{4,3,1,0,2:T(2,128)}), f32[16,2,16,2,256]{4,3,1,0,2:T(2,128)S(1)}, u32[]{:S(2)}, u32[]{:S(2)}) async-start(f32[16,2,16,2,256]{4,3,1,0,2:T(2,128)} %copy.263), calls=%async_computation.5 | async-start | bytes 2097152 | tf_op jit(solution)/shard_map/all_to_all | solution.py:179
  425.5 16.5 %all-to-all-done.5 = f32[16,2,16,2,256]{4,3,1,0,2:T(2,128)S(1)} async-done(((f32[16,2,16,2,256]{4,3,1,0,2:T(2,128)}), f32[16,2,16,2,256]{4,3,1,0,2:T(2,128)S(1)}, u32[]{:S(2)}, u32[]{:S(2)}) %all-to-all-start.5) | async-done | bytes 1048608 | tf_op jit(solution)/shard_map/all_to_all | solution.py:179
  442.6 4.9 reshape.1658
  447.4 5.0 broadcast.507
  452.4 124.1 %scatter_fusion.4 = f32[1600,16,16]{2,1,0:T(8,128)} fusion(f32[1600,16,16]{2,1,0:T(8,128)} %broadcast.507, s32[1024]{0:T(1024)S(1)} %reshape.1656, f32[1024,16,16]{2,1,0:T(8,128)} %reshape.1658), kind=kCustom, calls=%fused_computation.35 | custom fusion | flops 262144 | bytes 3149824
  576.6 15.1 %copy.266 = f32[40,16,40,16]{3,2,1,0:T(8,128)} copy(f32[40,16,40,16]{3,1,2,0:T(8,128)} %bitcast.378) | data formatting | bytes 3276800 | tf_op jit(solution)/shard_map/scatter-add | solution.py:186
  591.7 8.3 %reshape.1373 = f32[640,640]{1,0:T(8,128)S(1)} reshape(f32[40,16,40,16]{3,2,1,0:T(8,128)} %copy.266) | data formatting | bytes 3276800 | tf_op jit(solution)/shard_map/reshape | solution.py:187
  (240 shorter events, 164.9 us)
Async XLA Ops:
  0.0 0.7 copy-start
  19.8 29.3 %all-to-all-start.1 = ((s32[16,16,4]{0,2,1:T(4,128)}), s32[16,16,4]{0,2,1:T(4,128)S(1)}, u32[]{:S(2)}, u32[]{:S(2)}) async-start(s32[16,16,4]{0,2,1:T(4,128)} %copy.229), calls=%async_computation.1 | async-start | bytes 65536 | tf_op jit(solution)/shard_map/all_to_all | solution.py:150
  74.4 4.4 copy-start.15
  74.4 30.8 %all-to-all-start.2 = ((f32[16,2,16,2,256]{4,3,2,1,0:T(2,128)}), f32[16,2,16,2,256]{4,3,2,1,0:T(2,128)S(1)}, u32[]{:S(2)}, u32[]{:S(2)}) async-start(f32[16,2,16,2,256]{4,3,2,1,0:T(2,128)} %reshape.1348), calls=%async_computation.2 | async-start | bytes 2097152 | tf_op jit(solution)/shard_map/all_to_all | solution.py:165
  86.5 34.5 %copy-start.11 = (f32[4,256,256]{2,1,0:T(8,128)S(1)}, f32[4,256,256]{2,1,0:T(8,128)}, u32[]{:S(2)}) copy-start(f32[4,256,256]{2,1,0:T(8,128)} %param.21) | copy-start | bytes 3145732
  106.7 142.0 %all-to-all-start.3 = ((f32[16,2,16,2,256]{4,3,1,0,2:T(2,128)}), f32[16,2,16,2,256]{4,3,1,0,2:T(2,128)}, u32[]{:S(2)}, u32[]{:S(2)}) async-start(f32[16,2,16,2,256]{4,3,1,0,2:T(2,128)} %copy.236), calls=%async_computation.3 | async-start | bytes 2097152 | tf_op jit(solution)/shard_map/all_to_all | solution.py:164
  122.6 6.7 %copy-start.6 = (f32[16,16,16,16]{3,2,1,0:T(8,128)}, f32[16,16,16,16]{3,2,1,0:T(8,128)S(1)}, u32[]{:S(2)}) copy-start(f32[16,16,16,16]{3,2,1,0:T(8,128)S(1)} %reshape_squeeze.12) | copy-start | bytes 786436
  134.9 6.6 %copy-start.5 = (f32[16,16,16,16]{3,2,1,0:T(8,128)}, f32[16,16,16,16]{3,2,1,0:T(8,128)S(1)}, u32[]{:S(2)}) copy-start(f32[16,16,16,16]{3,2,1,0:T(8,128)S(1)} %reshape_squeeze.13) | copy-start | bytes 786436
  147.4 6.6 %copy-start.4 = (f32[16,16,16,16]{3,2,1,0:T(8,128)}, f32[16,16,16,16]{3,2,1,0:T(8,128)S(1)}, u32[]{:S(2)}) copy-start(f32[16,16,16,16]{3,2,1,0:T(8,128)S(1)} %reshape_squeeze.14) | copy-start | bytes 786436
  166.5 1.9 copy-start.14
  175.5 4.4 copy-start.7
  186.0 6.4 %copy-start.16 = (f32[1,512]{1,0:T(1,128)S(1)}, f32[1,512]{1,0:T(1,128)}, u32[]{:S(2)}) copy-start(f32[1,512]{1,0:T(1,128)} %param.28) | copy-start | bytes 6148
  189.1 6.8 %copy-start.2 = (s32[1,512]{1,0:T(1,128)S(1)}, s32[1,512]{1,0:T(1,128)}, u32[]{:S(2)}) copy-start(s32[1,512]{1,0:T(1,128)} %param.25) | copy-start | bytes 6148
  192.4 7.1 %copy-start.3 = (s32[1,512]{1,0:T(1,128)S(1)}, s32[1,512]{1,0:T(1,128)}, u32[]{:S(2)}) copy-start(s32[1,512]{1,0:T(1,128)} %param.26) | copy-start | bytes 6148
  248.7 2.6 copy-start.9
  326.8 1.2 copy-start.8
  415.5 9.3 %copy-start.13 = (s32[16,2,16]{0,1,2:T(2,128)S(1)}, s32[16,2,16]{0,1,2:T(2,128)}, u32[]{:S(2)}) copy-start(s32[16,2,16]{0,1,2:T(2,128)} %get-tuple-element.1252) | copy-start | bytes 6148
  415.5 9.4 %copy-start.12 = (s32[16,16,2]{0,2,1:T(2,128)S(1)}, s32[16,16,2]{0,2,1:T(2,128)}, u32[]{:S(2)}) copy-start(s32[16,16,2]{0,2,1:T(2,128)} %get-tuple-element.1254) | copy-start | bytes 6148
  415.5 9.5 %copy-start.17 = (s32[2]{0:T(128)S(1)}, s32[2]{0:T(128)}, u32[]{:S(2)}) copy-start(s32[2]{0:T(128)} %constant.558) | copy-start | bytes 28
  417.0 25.0 %all-to-all-start.5 = ((f32[16,2,16,2,256]{4,3,1,0,2:T(2,128)}), f32[16,2,16,2,256]{4,3,1,0,2:T(2,128)S(1)}, u32[]{:S(2)}, u32[]{:S(2)}) async-start(f32[16,2,16,2,256]{4,3,1,0,2:T(2,128)} %copy.263), calls=%async_computation.5 | async-start | bytes 2097152 | tf_op jit(solution)/shard_map/all_to_all | solution.py:179
  591.7 8.3 %copy-start.10 = (f32[640,640]{1,0:T(8,128)S(1)}, f32[640,640]{1,0:T(8,128)}, u32[]{:S(2)}) copy-start(f32[640,640]{1,0:T(8,128)} %param.20) | copy-start | bytes 4915204
  591.7 9.6 %copy-start.1 = (s32[640]{0:T(1024)S(1)}, s32[640]{0:T(1024)}, u32[]{:S(2)}) copy-start(s32[640]{0:T(1024)} %param.23) | copy-start | bytes 7684
where the time goes:
time: 612 us; the launch traced here: 602 us
  local copies, waits for them, and re-layouts  227 us (37%)
  other arithmetic  162 us (26%)
  blocking collectives  104 us (17%)
  waiting for transfers between devices  35.2 us (6%)
  starting transfers between devices  30.2 us (5%)
  matrix products  28.6 us (5%)
  between operations  14 us (2%)
    unnamed x4, other arithmetic  124 us
    all_to_all x1, blocking collectives, on_device(): lax.all_to_all(outbound, 'row', split_axis=0, concat_axis=0, tiled=True)  86.3 us
    reshape x24, local copies, waits for them, and re-layouts, make_class_stacks(): tables.append(jnp.transpose(tensor, single).reshape(pair_width, pair_width))  61.1 us
    another operation x20, local copies, waits for them, and re-layouts, make_class_stacks(): tensor = class_tables[klass].reshape(SHELL, SHELL, SHELL, SHELL)  36.9 us
    dot_general x24, matrix products, class_terms(): product = jnp.dot(scaled[source], table, precision=lax.Precision.HIGHEST)  28.6 us
    scatter-add x4, other arithmetic, block_step(): return running.at[targets].add(values)  25.8 us
    reshape x2, local copies, waits for them, and re-layouts, on_device(): density_view = density.reshape(row_blocks, SHELL, col_blocks, SHELL)  20.5 us
    all_to_all x1, waiting for transfers between devices, on_device(): lax.all_to_all(picked, 'row', split_axis=0, concat_axis=0, tiled=True)  18.7 us
  transfers between devices with their start and end apart: 4, of which 2 were waited for; matrix products, arithmetic and copies ran while one was open for 25% of the time, Pallas kernels for 0%

commit v1 on v0

v1 whole, which is shorter than its diff:
```python
import functools

import jax
import jax.numpy as jnp
from jax import lax
from jax.experimental import pallas as pl
from jax.experimental.pallas import tpu as pltpu
from jax.sharding import PartitionSpec as P

SHELL = 16
LANES = 128
SUBLANES = 8
GROUPS = LANES // SHELL
AXES = ("row", "col")
NT = (((1,), (1,)), ((), ()))
NN = (((1,), (0,)), ((), ()))
TN = (((0,), (0,)), ((), ()))


def swap_groups(tile):
    sublane = lax.broadcasted_iota(jnp.int32, tile.shape, 0)
    group = lax.broadcasted_iota(jnp.int32, tile.shape, 1) // SHELL
    for bit in (1, 2, 4):
        low = (sublane & bit) == 0
        left = (group & bit) == 0
        down = pltpu.roll(pltpu.roll(tile, bit, 0), LANES - SHELL * bit, 1)
        if 2 * bit == SUBLANES:
            tile = jnp.where(low == left, tile, down)
        else:
            up = pltpu.roll(pltpu.roll(tile, SUBLANES - bit, 0), SHELL * bit, 1)
            tile = jnp.where(low == left, tile, jnp.where(low, up, down))
    return tile


def split(values):
    high = values.astype(jnp.bfloat16)
    low = (values - high.astype(jnp.float32)).astype(jnp.bfloat16)
    return high, low


def dot(left, right, dims):
    return lax.dot_general(left, right, dims, preferred_element_type=jnp.float32)


def pick_kernel(wanted_ref, density_ref, out_ref, flat_ref):
    row_blocks = density_ref.shape[0] // SHELL
    col_blocks = density_ref.shape[1] // SHELL
    devices = out_ref.shape[0] // SUBLANES

    def flatten(block, carry):
        for half in range(2):
            start = pl.multiple_of(block * SHELL + half * SUBLANES, SUBLANES)
            for tile in range(col_blocks // GROUPS):
                lanes = slice(tile * LANES, (tile + 1) * LANES)
                values = density_ref[pl.ds(start, SUBLANES), lanes]
                place = (block * col_blocks + tile * GROUPS) * 2 + half
                flat_ref[pl.ds(place, SUBLANES, stride=2), :] = swap_groups(values)
        return carry

    lax.fori_loop(0, row_blocks, flatten, 0)

    def pick(device, carry):
        for part in range(4):
            block = wanted_ref[4 * device + part // 2] * col_blocks + wanted_ref[4 * device + 2 + part % 2]
            source = pl.multiple_of(2 * block, 2)
            target = pl.multiple_of(SUBLANES * device + 2 * part, 2)
            out_ref[pl.ds(target, 2), :] = flat_ref[pl.ds(source, 2), :]
        return carry

    lax.fori_loop(0, devices, pick, 0, unroll=4)


def pick_blocks(wanted, density, devices):
    blocks = (density.shape[0] // SHELL) * (density.shape[1] // SHELL)
    return pl.pallas_call(
        pick_kernel,
        out_shape=jax.ShapeDtypeStruct((devices * SUBLANES, LANES), jnp.float32),
        in_specs=[
            pl.BlockSpec(memory_space=pltpu.SMEM),
            pl.BlockSpec(memory_space=pltpu.VMEM),
        ],
        out_specs=pl.BlockSpec(memory_space=pltpu.VMEM),
        scratch_shapes=[pltpu.VMEM((2 * blocks, LANES), jnp.float32)],
        compiler_params=pltpu.CompilerParams(vmem_limit_bytes=40 << 20),
        name="pick_blocks",
    )(wanted, density)


def merge_kernel(wanted_ref, parts_ref, core_ref, out_ref, flat_ref):
    row_blocks = core_ref.shape[0] // SHELL
    col_blocks = core_ref.shape[1] // SHELL
    devices = parts_ref.shape[0] // SUBLANES
    flat_ref[...] = jnp.zeros_like(flat_ref)

    def add(device, carry):
        places = []
        sums = []
        for part in range(4):
            block = wanted_ref[4 * device + part // 2] * col_blocks + wanted_ref[4 * device + 2 + part % 2]
            place = pl.ds(pl.multiple_of(2 * block, 2), 2)
            source = pl.multiple_of(SUBLANES * device + 2 * part, 2)
            places.append(place)
            sums.append(flat_ref[place, :] + parts_ref[pl.ds(source, 2), :])
        for place, value in zip(places, sums):
            flat_ref[place, :] = value
        return carry

    lax.fori_loop(0, devices, add, 0, unroll=4)

    def unflatten(block, carry):
        for half in range(2):
            start = pl.multiple_of(block * SHELL + half * SUBLANES, SUBLANES)
            for tile in range(col_blocks // GROUPS):
                lanes = slice(tile * LANES, (tile + 1) * LANES)
                place = (block * col_blocks + tile * GROUPS) * 2 + half
                values = swap_groups(flat_ref[pl.ds(place, SUBLANES, stride=2), :])
                out_ref[pl.ds(start, SUBLANES), lanes] = core_ref[pl.ds(start, SUBLANES), lanes] + values
        return carry

    lax.fori_loop(0, row_blocks, unflatten, 0)


def merge_blocks(wanted, parts, core):
    blocks = (core.shape[0] // SHELL) * (core.shape[1] // SHELL)
    return pl.pallas_call(
        merge_kernel,
        out_shape=jax.ShapeDtypeStruct(core.shape, jnp.float32),
        in_specs=[
            pl.BlockSpec(memory_space=pltpu.SMEM),
            pl.BlockSpec(memory_space=pltpu.VMEM),
            pl.BlockSpec(memory_space=pltpu.VMEM),
        ],
        out_specs=pl.BlockSpec(memory_space=pltpu.VMEM),
        scratch_shapes=[pltpu.VMEM((2 * blocks, LANES), jnp.float32)],
        compiler_params=pltpu.CompilerParams(vmem_limit_bytes=40 << 20),
        name="merge_blocks",
    )(wanted, parts, core)


def table_kernel(tables_ref, out_ref, mid_ref, turned_ref, last_ref):
    table = tables_ref[0]
    width = table.shape[0]
    halves = range(2)
    high, low = split(table)
    out_ref[0, 0, 0] = high
    out_ref[0, 0, 1] = low

    def swap_inner(first, carry):
        for a in halves:
            for b in halves:
                rows = pl.ds(pl.multiple_of(first * SHELL + SUBLANES * a, SUBLANES), SUBLANES)
                values = tables_ref[0, rows, LANES * b:LANES * (b + 1)]
                rows = pl.ds(pl.multiple_of(first * SHELL + SUBLANES * b, SUBLANES), SUBLANES)
                mid_ref[rows, LANES * a:LANES * (a + 1)] = swap_groups(values)
        return carry

    lax.fori_loop(0, width // SHELL, swap_inner, 0)
    high, low = split(mid_ref[...])
    out_ref[0, 1, 0] = high
    out_ref[0, 1, 1] = low
    turned = mid_ref[...].T
    for b in halves:
        turned_ref[b] = turned[:, LANES * b:LANES * (b + 1)]

    def swap_outer(last, carry):
        for a in halves:
            for b in halves:
                rows = pl.ds(LANES * a + last, SUBLANES, stride=SHELL)
                values = turned_ref[b, rows, :]
                rows = pl.ds(LANES * b + last, SUBLANES, stride=SHELL)
                last_ref[a, rows, :] = swap_groups(values)
        return carry

    lax.fori_loop(0, SHELL, swap_outer, 0)
    for a in halves:
        high, low = split(last_ref[a])
        out_ref[0, 2, 0, :, LANES * a:LANES * (a + 1)] = high
        out_ref[0, 2, 1, :, LANES * a:LANES * (a + 1)] = low


def make_tables(class_tables):
    classes, width, _ = class_tables.shape
    return pl.pallas_call(
        table_kernel,
        grid=(classes,),
        out_shape=jax.ShapeDtypeStruct((classes, 3, 2, width, width), jnp.bfloat16),
        in_specs=[pl.BlockSpec((1, width, width), lambda c: (c, 0, 0))],
        out_specs=pl.BlockSpec((1, 3, 2, width, width), lambda c: (c, 0, 0, 0, 0)),
        scratch_shapes=[
            pltpu.VMEM((width, width), jnp.float32),
            pltpu.VMEM((2, width, LANES), jnp.float32),
            pltpu.VMEM((2, width, LANES), jnp.float32),
        ],
        compiler_params=pltpu.CompilerParams(vmem_limit_bytes=40 << 20),
        name="make_tables",
    )(class_tables)


def quartet_kernel(
    count_ref, blocks_ref, left_ref, right_ref, columns_ref, rows_ref, weights_ref, tables_ref,
    out_ref, scaled_ref, pieces_ref, totals_ref,
):
    slots, classes = weights_ref.shape
    pairs = pieces_ref.shape[0]
    width = totals_ref.shape[1]
    step_rows = 128
    scaled_ref[...] = (blocks_ref[...].reshape(16, 16, SUBLANES, LANES) * left_ref[...][:, None]
                       * right_ref[...][None]).reshape(scaled_ref.shape)
    for half in range(2):
        high, low = split(scaled_ref[pl.ds(half, pairs, stride=2), :])
        pieces_ref[:, LANES * half:LANES * (half + 1)] = high
        pieces_ref[:, width + LANES * half:width + LANES * (half + 1)] = low
    totals_ref[...] = jnp.zeros_like(totals_ref)

    def step(index, carry):
        here = pl.ds(pl.multiple_of(index * step_rows, step_rows), step_rows)
        lane = lax.broadcasted_iota(jnp.int32, (step_rows, pairs), 1)
        weights = weights_ref[here, :]
        values_high = []
        values_low = []
        for kind in range(6):
            column = columns_ref[here, kind:kind + 1]
            chosen = jnp.where(lane == column, 1.0, 0.0).astype(jnp.bfloat16)
            found = dot(chosen, pieces_ref[...], NN).astype(jnp.bfloat16)
            high, low = found[:, :width], found[:, width:]
            form = kind // 2
            dims = NT if kind % 2 == 0 else NN
            total = jnp.zeros((step_rows, width), jnp.float32)
            for klass in range(classes):
                product = dot(high, tables_ref[klass, form, 0], dims)
                product += dot(high, tables_ref[klass, form, 1], dims)
                product += dot(low, tables_ref[klass, form, 0], dims)
                total += product * weights[:, klass:klass + 1]
            if kind >= 2:
                total = total * -0.5
            high, low = split(total)
            values_high.append(high)
            values_low.append(low)
        sublane = lax.broadcasted_iota(jnp.int32, (pairs, step_rows), 0)
        sums = totals_ref[...]
        for kind in range(6):
            row = rows_ref[kind ^ 1:(kind ^ 1) + 1, here]
            chosen = jnp.where(sublane == row, 1.0, 0.0).astype(jnp.bfloat16)
            sums += dot(chosen, values_high[kind], NN) + dot(chosen, values_low[kind], NN)
        totals_ref[...] = sums
        return carry

    lax.fori_loop(0, (count_ref[0] + step_rows - 1) // step_rows, step, 0)
    for half in range(2):
        scaled_ref[pl.ds(half, pairs, stride=2), :] = totals_ref[:, LANES * half:LANES * (half + 1)]
    out_ref[...] = (scaled_ref[...].reshape(16, 16, SUBLANES, LANES) * left_ref[...][:, None]
                    * right_ref[...][None]).reshape(out_ref.shape)


def add_quartets(count, blocks, left, right, columns, rows, weights, tables):
    lines = blocks.shape[0]
    width = tables.shape[-1]
    vmem = pl.BlockSpec(memory_space=pltpu.VMEM)
    return pl.pallas_call(
        quartet_kernel,
        out_shape=jax.ShapeDtypeStruct(blocks.shape, jnp.float32),
        in_specs=[pl.BlockSpec(memory_space=pltpu.SMEM)] + [vmem] * 7,
        out_specs=vmem,
        scratch_shapes=[
            pltpu.VMEM((lines, LANES), jnp.float32),
            pltpu.VMEM((lines // 2, 2 * width), jnp.bfloat16),
            pltpu.VMEM((lines // 2, width), jnp.float32),
        ],
        compiler_params=pltpu.CompilerParams(vmem_limit_bytes=56 << 20),
        name="add_quartets",
    )(count, blocks, left, right, columns, rows, weights, tables)


def exchange(values):
    return lax.all_to_all(values, AXES, split_axis=0, concat_axis=0, tiled=True)


def on_device(
    density,
    core_hamiltonian,
    class_tables,
    shell_scale,
    block_place,
    work_blocks,
    quartet_bra,
    quartet_ket,
    quartet_class,
    quartet_factor,
    quartet_count,
):
    row_count = lax.axis_size("row")
    col_count = lax.axis_size("col")
    devices = row_count * col_count
    task_count = work_blocks.shape[1]
    row_blocks = density.shape[0] // SHELL
    col_blocks = density.shape[1] // SHELL
    classes = class_tables.shape[0]
    own_tasks = work_blocks[0]
    places = block_place[own_tasks]
    row_part = (places % row_blocks).reshape(row_count, 2)
    col_part = (places % col_blocks).reshape(col_count, 2)
    outgoing = jnp.concatenate(
        (
            jnp.broadcast_to(row_part[:, None, :], (row_count, col_count, 2)),
            jnp.broadcast_to(col_part[None, :, :], (row_count, col_count, 2)),
        ),
        axis=2,
    )
    wanted = exchange(outgoing.reshape(devices, 4)).reshape(devices * 4)
    picked = pick_blocks(wanted, density, devices)
    blocks = exchange(picked.reshape(devices, SUBLANES, LANES))
    blocks = blocks.reshape(devices * SUBLANES, LANES)

    tables = make_tables(class_tables)
    scales = shell_scale.reshape(-1, SHELL)[own_tasks]
    left = jnp.broadcast_to(
        scales.reshape(row_count, 2, 1, 2, SUBLANES, 1), (row_count, 2, 2, 2, SUBLANES, SHELL)
    ).reshape(row_count, SUBLANES, LANES)
    right = jnp.broadcast_to(
        scales.reshape(col_count, 1, 2, 1, 1, SHELL), (col_count, 2, 2, 2, SUBLANES, SHELL)
    ).reshape(col_count, SUBLANES, LANES)
    bra, ket = quartet_bra[0], quartet_ket[0]
    shell_a, shell_b = bra // task_count, bra % task_count
    shell_c, shell_d = ket // task_count, ket % task_count

    def line(first, second):
        return ((first // 2) * col_count + second // 2) * 4 + (first % 2) * 2 + second % 2

    rows = jnp.stack(
        (
            line(shell_c, shell_d),
            line(shell_a, shell_b),
            line(shell_b, shell_d),
            line(shell_a, shell_c),
            line(shell_b, shell_c),
            line(shell_a, shell_d),
        )
    )
    slots = rows.shape[1]
    live = jnp.where(jnp.arange(slots) < quartet_count[0], quartet_factor[0], 0.0)
    weights = jnp.where(quartet_class[0][:, None] == jnp.arange(classes)[None, :], live[:, None], 0.0)
    summed = add_quartets(quartet_count, blocks, left, right, rows.T, rows, weights, tables)
    returned = exchange(summed.reshape(devices, SUBLANES, LANES))
    return merge_blocks(wanted, returned.reshape(devices * SUBLANES, LANES), core_hamiltonian)


def solution(mesh):
    placed = (
        P("row", "col"),
        P("row", "col"),
        P(),
        P(),
        P(),
        P(("row", "col"), None),
        P(("row", "col"), None),
        P(("row", "col"), None),
        P(("row", "col"), None),
        P(("row", "col"), None),
        P(("row", "col")),
    )
    return jax.shard_map(
        on_device, mesh=mesh, in_specs=placed, out_specs=P("row", "col"), check_vma=False
    )
```

time: 612 us -> 175 us (0.29); the launches traced: 602 us -> 175 us
  local copies, waits for them, and re-layouts: 227 us -> 9.24 us
  other arithmetic: 162 us -> 2.74 us
  Pallas kernels: 0 us -> 65.2 us
  waiting for transfers between devices: 35.2 us -> 0.01 us
  matrix products: 28.6 us -> 0 us
  starting transfers between devices: 30.2 us -> 5.6 us
  between operations: 14 us -> 0.9 us
  blocking collectives: 104 us -> 91.1 us
    unnamed x4 -> x0, other arithmetic: 124 us -> none
    reshape x32 -> x4, local copies, waits for them, and re-layouts: 104 us -> 1.86 us  [the longest x1 0.8 us: on_device(): right = jnp.broadcast_to(scales.reshape(col_count, 1, 2, 1, 1, SHELL), (c...]
    pallas_call x0 -> x4, Pallas kernels: none -> 65.2 us  [the longest x1 29.4 us: make_tables(): pl.pallas_call(table_kernel, grid=(classes,), out_shape=jax.ShapeDtypeStr...]
    gather x31 -> x1, local copies, waits for them, and re-layouts: 48.9 us -> 0.57 us  [on_device(): scales = shell_scale.reshape(-1, SHELL)[own_tasks]]
    another operation x21 -> x1, local copies, waits for them, and re-layouts: 37.9 us -> 0.03 us  [on_device(): jnp.stack((line(shell_c, shell_d), line(shell_a, shell_b), line(shell_b,...]
    all_to_all x4 -> x1, waiting for transfers between devices: 35.2 us -> 0.01 us  [exchange(): return lax.all_to_all(values, AXES, split_axis=0, concat_axis=0, tiled=True)]
    dot_general x24 -> x0, matrix products: 28.6 us -> none  [class_terms(): product = jnp.dot(scaled[source], table, precision=lax.Precision.HIGHEST)]
    scatter-add x4 -> x0, other arithmetic: 25.8 us -> none  [block_step(): return running.at[targets].add(values)]
  transfers between devices with their start and end apart: 4 -> 1, of which waited for: 2 -> 0; matrix products, arithmetic and copies ran while one was open for 25% -> 3% of each run, Pallas kernels for 0% -> 17%
where the time goes in v1:
time: 175 us
  blocking collectives  91.1 us (52%)
  Pallas kernels  65.2 us (37%)
  local copies, waits for them, and re-layouts  9.24 us (5%)
  starting transfers between devices  5.6 us (3%)
  other arithmetic  2.74 us (2%)
    all_to_all x2, blocking collectives, exchange(): return lax.all_to_all(values, AXES, split_axis=0, concat_axis=0, tiled=True)  91.1 us
    pallas_call x1, Pallas kernels, make_tables(): pl.pallas_call(table_kernel, grid=(classes,), out_shape=jax.ShapeDtypeStr...  29.4 us
    pallas_call x1, Pallas kernels, merge_blocks(): pl.pallas_call(merge_kernel, out_shape=jax.ShapeDtypeStruct(core.shape, j...  13.3 us
    pallas_call x1, Pallas kernels, pick_blocks(): pl.pallas_call(pick_kernel, out_shape=jax.ShapeDtypeStruct((devices * SUB...  13.1 us
    pallas_call x1, Pallas kernels, add_quartets(): pl.pallas_call(quartet_kernel, out_shape=jax.ShapeDtypeStruct(blocks.shap...  9.53 us
    all_to_all x1, starting transfers between devices, exchange(): return lax.all_to_all(values, AXES, split_axis=0, concat_axis=0, tiled=True)  5.6 us
    unnamed x24, local copies, waits for them, and re-layouts  4.07 us
  transfers between devices with their start and end apart: 1, of which 0 were waited for; matrix products, arithmetic and copies ran while one was open for 3% of the time, Pallas kernels for 17%

profile of v1, /device:TPU:1, one launch (start us, length us, event | category | flops | bytes accessed | tf_op | source)
XLA Modules:
  0.0 174.9 jit_solution(2612546919858151755)
XLA Ops:
  0.0 0.7 fusion.4
  0.7 0.0 copy-done
  0.7 0.7 gather_fusion
  1.4 0.1 rem.181
  1.5 0.1 copy.14
  1.6 0.1 broadcast_in_dim.44
  1.6 0.2 copy.16
  1.8 28.6 %all_to_all.19 = s32[256,1,4]{2,1,0:T(1,128)S(1)} all-to-all(s32[256,1,4]{2,1,0:T(1,128)S(1)} %bitcast.22), channel_id=1, replica_groups=mesh['row'=16,'col'=16] {'row','col'}, dimensions={0} | all-to-all | bytes 8192 | tf_op jit(solution)/shard_map/all_to_all | solution.py:275
  30.4 0.5 broadcast.457
  31.0 1.0 reduce.3
  31.9 0.1 reshape.93.wanted_ref
  32.0 0.0 copy-start.3
  32.1 1.4 copy-done.3
  33.5 13.1 %pick_blocks.1 = f32[2048,128]{1,0:T(8,128)} custom-call(s32[1024]{0:T(1024)S(1)} %reshape.93.wanted_ref, f32[640,640]{1,0:T(8,128)S(1)} %copy-done.3), custom_call_target="tpu_custom_call" | custom-call | tf_op jit(solution)/shard_map/pick_blocks/pallas_call | solution.py:75
  46.5 5.6 %all-to-all-start.1 = ((f32[256,8,128]{2,1,0:T(8,128)}), f32[256,8,128]{2,1,0:T(8,128)S(1)}, u32[]{:S(2)}, u32[]{:S(2)}) async-start(f32[256,8,128]{2,1,0:T(8,128)} %bitcast.3), calls=%async_computation.1 | async-start | bytes 2097152 | tf_op jit(solution)/shard_map/all_to_all | solution.py:275
  52.1 0.0 copy-start.4
  53.0 0.1 add_add_fusion.1
  53.1 0.9 copy.17.columns_ref
  54.0 0.1 reshape.96
  54.1 0.6 gather_fusion.1
  54.7 0.1 broadcast_in_dim.46
  54.8 0.1 broadcast_in_dim.47
  54.9 0.8 reshape.97.left_ref
  55.8 0.8 reshape.98.right_ref
  56.6 29.4 %make_tables.1.tables_ref = bf16[4,3,2,256,256]{4,3,2,1,0:T(8,128)(2,1)S(1)} custom-call(f32[4,256,256]{2,1,0:T(8,128)S(1)} %copy-done.4), custom_call_target="tpu_custom_call" | custom-call | tf_op jit(solution)/shard_map/make_tables/pallas_call | solution.py:183
  86.0 1.6 copy-done.1
  87.7 0.9 fusion.weights_ref
  88.6 0.0 all-to-all-done.1
  88.6 1.0 copy-done.5
  89.6 9.5 %add_quartets.1 = f32[2048,128]{1,0:T(8,128)} custom-call(s32[1]{0:T(128)} %copy.18.count_ref, f32[2048,128]{1,0:T(8,128)} %bitcast.20, f32[16,8,128]{2,1,0:T(8,128)} %reshape.97.left_ref, f32[16,8,128]{2,1,0:T(8,128)} %reshape.98.right_ref, s32[512,6]{1,0:T(8,128)} %copy.17.columns_ref, s32[6,512]{1,0:T(8,128)} %copy-done.6, f32[512,4]{1,0:T(8,128)} %fusion.weights_ref, ...), custom_call_target="tpu_custom_call" | custom-call | tf_op jit(solution)/shard_map/add_quartets/pallas_call | solution.py:259
  99.1 62.5 %all_to_all.20 = f32[256,8,128]{2,1,0:T(8,128)S(1)} all-to-all(f32[256,8,128]{2,1,0:T(8,128)} %bitcast.21), channel_id=1, replica_groups=mesh['row'=16,'col'=16] {'row','col'}, dimensions={0} | all-to-all | bytes 2097152 | tf_op jit(solution)/shard_map/all_to_all | solution.py:275
  161.6 13.3 %merge_blocks.1 = f32[640,640]{1,0:T(8,128)} custom-call(s32[1024]{0:T(1024)S(1)} %reshape.93.wanted_ref, f32[2048,128]{1,0:T(8,128)S(1)} %bitcast.19, f32[640,640]{1,0:T(8,128)S(1)} %copy-done.2), custom_call_target="tpu_custom_call" | custom-call | tf_op jit(solution)/shard_map/merge_blocks/pallas_call | solution.py:125
  (29 shorter events, 0.3 us)
Async XLA Ops:
  0.0 0.7 copy-start
  32.0 1.4 copy-start.3
  46.5 6.4 %copy-start.10 = (s32[1,512]{1,0:T(1,128)S(1)}, s32[1,512]{1,0:T(1,128)}, u32[]{:S(2)}) copy-start(s32[1,512]{1,0:T(1,128)} %param.17) | copy-start | bytes 6148
  46.5 6.4 %copy-start.8 = (s32[1,512]{1,0:T(1,128)S(1)}, s32[1,512]{1,0:T(1,128)}, u32[]{:S(2)}) copy-start(s32[1,512]{1,0:T(1,128)} %param.18) | copy-start | bytes 6148
  46.5 7.4 %copy-start.7 = (f32[10240]{0:T(1024)S(1)}, f32[10240]{0:T(1024)}, u32[]{:S(2)}) copy-start(f32[10240]{0:T(1024)} %param.14) | copy-start | bytes 122884
  46.5 42.0 %all-to-all-start.1 = ((f32[256,8,128]{2,1,0:T(8,128)}), f32[256,8,128]{2,1,0:T(8,128)S(1)}, u32[]{:S(2)}, u32[]{:S(2)}) async-start(f32[256,8,128]{2,1,0:T(8,128)} %bitcast.3), calls=%async_computation.1 | async-start | bytes 2097152 | tf_op jit(solution)/shard_map/all_to_all | solution.py:275
  52.1 4.4 %copy-start.4 = (f32[4,256,256]{2,1,0:T(8,128)S(1)}, f32[4,256,256]{2,1,0:T(8,128)}, u32[]{:S(2)}) copy-start(f32[4,256,256]{2,1,0:T(8,128)} %tables_ref.1) | copy-start | bytes 3145732
  53.1 32.9 %copy-start.6 = (s32[6,512]{1,0:T(8,128)}, s32[6,512]{1,0:T(8,128)S(1)}, u32[]{:S(2)}) copy-start(s32[6,512]{1,0:T(8,128)S(1)} %stack.2.rows_ref) | copy-start | bytes 36868
  56.6 31.1 %copy-start.11 = (f32[1,512]{1,0:T(1,128)S(1)}, f32[1,512]{1,0:T(1,128)}, u32[]{:S(2)}) copy-start(f32[1,512]{1,0:T(1,128)} %param.20) | copy-start | bytes 6148
  56.6 31.1 %copy-start.9 = (s32[1,512]{1,0:T(1,128)S(1)}, s32[1,512]{1,0:T(1,128)}, u32[]{:S(2)}) copy-start(s32[1,512]{1,0:T(1,128)} %param.19) | copy-start | bytes 6148
  86.0 1.6 copy-start.1
  88.6 1.0 copy-start.5
  99.1 62.5 %copy-start.2 = (f32[640,640]{1,0:T(8,128)S(1)}, f32[640,640]{1,0:T(8,128)}, u32[]{:S(2)}) copy-start(f32[640,640]{1,0:T(8,128)} %core_ref.1) | copy-start | bytes 4915204

commit v2 on v1

v2 whole, which is shorter than its diff:
```python
import functools

import jax
import jax.numpy as jnp
from jax import lax
from jax.experimental import pallas as pl
from jax.experimental.pallas import tpu as pltpu
from jax.sharding import PartitionSpec as P

SHELL = 16
LANES = 128
SUBLANES = 8
GROUPS = LANES // SHELL
AXES = ("row", "col")
NT = (((1,), (1,)), ((), ()))
NN = (((1,), (0,)), ((), ()))


def swap_groups(tile):
    sublane = lax.broadcasted_iota(jnp.int32, tile.shape, 0)
    lane = lax.broadcasted_iota(jnp.int32, tile.shape, 1)
    group, inner = lane // SHELL, lane % SHELL
    tile = jnp.take_along_axis(tile, ((sublane + group) % GROUPS) * SHELL + inner, axis=1)
    tile = jnp.take_along_axis(tile, (sublane - group) % SUBLANES, axis=0)
    return jnp.take_along_axis(tile, ((sublane - group) % GROUPS) * SHELL + inner, axis=1)


def split(values):
    high = values.astype(jnp.bfloat16)
    low = (values - high.astype(jnp.float32)).astype(jnp.bfloat16)
    return high, low


def dot(left, right, dims):
    return lax.dot_general(left, right, dims, preferred_element_type=jnp.float32)


def flatten_kernel(density_ref, flat_ref):
    row_blocks = density_ref.shape[0] // SHELL
    col_blocks = density_ref.shape[1] // SHELL

    def flatten(block, carry):
        for half in range(2):
            start = pl.multiple_of(block * SHELL + half * SUBLANES, SUBLANES)
            for tile in range(col_blocks // GROUPS):
                lanes = slice(tile * LANES, (tile + 1) * LANES)
                values = density_ref[pl.ds(start, SUBLANES), lanes]
                place = (block * col_blocks + tile * GROUPS) * 2 + half
                flat_ref[pl.ds(place, SUBLANES, stride=2), :] = swap_groups(values)
        return carry

    lax.fori_loop(0, row_blocks, flatten, 0, unroll=8)


def flatten_blocks(density):
    blocks = (density.shape[0] // SHELL) * (density.shape[1] // SHELL)
    return pl.pallas_call(
        flatten_kernel,
        out_shape=jax.ShapeDtypeStruct((2 * blocks, LANES), jnp.float32),
        name="flatten_blocks",
    )(density)


def pick_kernel(wanted_ref, flat_ref, out_ref):
    def pick(device, carry):
        for part in range(4):
            source = pl.multiple_of(wanted_ref[4 * device + part // 2] + wanted_ref[4 * device + 2 + part % 2], 2)
            target = pl.multiple_of(SUBLANES * device + 2 * part, 2)
            out_ref[pl.ds(target, 2), :] = flat_ref[pl.ds(source, 2), :]
        return carry

    lax.fori_loop(0, out_ref.shape[0] // SUBLANES, pick, 0, unroll=8)


def pick_blocks(wanted, flat, devices):
    return pl.pallas_call(
        pick_kernel,
        out_shape=jax.ShapeDtypeStruct((devices * SUBLANES, LANES), jnp.float32),
        in_specs=[
            pl.BlockSpec(memory_space=pltpu.SMEM),
            pl.BlockSpec(memory_space=pltpu.VMEM),
        ],
        out_specs=pl.BlockSpec(memory_space=pltpu.VMEM),
        name="pick_blocks",
    )(wanted, flat)


def merge_kernel(wanted_ref, parts_ref, core_ref, out_ref, flat_ref):
    row_blocks = core_ref.shape[0] // SHELL
    col_blocks = core_ref.shape[1] // SHELL
    devices = parts_ref.shape[0] // SUBLANES
    flat_ref[...] = jnp.zeros_like(flat_ref)

    def add(device, carry):
        places = []
        sums = []
        for part in range(4):
            place = wanted_ref[4 * device + part // 2] + wanted_ref[4 * device + 2 + part % 2]
            place = pl.ds(pl.multiple_of(place, 2), 2)
            source = pl.multiple_of(SUBLANES * device + 2 * part, 2)
            places.append(place)
            sums.append(flat_ref[place, :] + parts_ref[pl.ds(source, 2), :])
        for place, value in zip(places, sums):
            flat_ref[place, :] = value
        return carry

    lax.fori_loop(0, devices, add, 0, unroll=8)

    def unflatten(block, carry):
        for half in range(2):
            start = pl.multiple_of(block * SHELL + half * SUBLANES, SUBLANES)
            for tile in range(col_blocks // GROUPS):
                lanes = slice(tile * LANES, (tile + 1) * LANES)
                place = (block * col_blocks + tile * GROUPS) * 2 + half
                values = swap_groups(flat_ref[pl.ds(place, SUBLANES, stride=2), :])
                out_ref[pl.ds(start, SUBLANES), lanes] = core_ref[pl.ds(start, SUBLANES), lanes] + values
        return carry

    lax.fori_loop(0, row_blocks, unflatten, 0, unroll=8)


def merge_blocks(wanted, parts, core):
    blocks = (core.shape[0] // SHELL) * (core.shape[1] // SHELL)
    return pl.pallas_call(
        merge_kernel,
        out_shape=jax.ShapeDtypeStruct(core.shape, jnp.float32),
        in_specs=[
            pl.BlockSpec(memory_space=pltpu.SMEM),
            pl.BlockSpec(memory_space=pltpu.VMEM),
            pl.BlockSpec(memory_space=pltpu.VMEM),
        ],
        out_specs=pl.BlockSpec(memory_space=pltpu.VMEM),
        scratch_shapes=[pltpu.VMEM((2 * blocks, LANES), jnp.float32)],
        compiler_params=pltpu.CompilerParams(vmem_limit_bytes=40 << 20),
        name="merge_blocks",
    )(wanted, parts, core)


def table_kernel(tables_ref, out_ref, mid_ref, turned_ref, last_ref):
    table = tables_ref[0]
    width = table.shape[0]
    halves = range(2)
    high, low = split(table)
    out_ref[0, 0, 0] = high
    out_ref[0, 0, 1] = low

    def swap_inner(first, carry):
        for a in halves:
            for b in halves:
                rows = pl.ds(pl.multiple_of(first * SHELL + SUBLANES * a, SUBLANES), SUBLANES)
                values = tables_ref[0, rows, LANES * b:LANES * (b + 1)]
                rows = pl.ds(pl.multiple_of(first * SHELL + SUBLANES * b, SUBLANES), SUBLANES)
                mid_ref[rows, LANES * a:LANES * (a + 1)] = swap_groups(values)
        return carry

    lax.fori_loop(0, width // SHELL, swap_inner, 0, unroll=4)
    high, low = split(mid_ref[...])
    out_ref[0, 1, 0] = high
    out_ref[0, 1, 1] = low
    turned = mid_ref[...].T
    for b in halves:
        turned_ref[b] = turned[:, LANES * b:LANES * (b + 1)]

    def swap_outer(last, carry):
        for a in halves:
            for b in halves:
                rows = pl.ds(LANES * a + last, SUBLANES, stride=SHELL)
                values = turned_ref[b, rows, :]
                rows = pl.ds(LANES * b + last, SUBLANES, stride=SHELL)
                last_ref[a, rows, :] = swap_groups(values)
        return carry

    lax.fori_loop(0, SHELL, swap_outer, 0, unroll=4)
    for a in halves:
        high, low = split(last_ref[a])
        out_ref[0, 2, 0, :, LANES * a:LANES * (a + 1)] = high
        out_ref[0, 2, 1, :, LANES * a:LANES * (a + 1)] = low


def make_tables(class_tables):
    classes, width, _ = class_tables.shape
    return pl.pallas_call(
        table_kernel,
        grid=(classes,),
        out_shape=jax.ShapeDtypeStruct((classes, 3, 2, width, width), jnp.bfloat16),
        in_specs=[pl.BlockSpec((1, width, width), lambda c: (c, 0, 0))],
        out_specs=pl.BlockSpec((1, 3, 2, width, width), lambda c: (c, 0, 0, 0, 0)),
        scratch_shapes=[
            pltpu.VMEM((width, width), jnp.float32),
            pltpu.VMEM((2, width, LANES), jnp.float32),
            pltpu.VMEM((2, width, LANES), jnp.float32),
        ],
        compiler_params=pltpu.CompilerParams(vmem_limit_bytes=40 << 20),
        name="make_tables",
    )(class_tables)


def sort_kernel(count_ref, bra_ref, ket_ref, class_ref, factor_ref, columns_ref, rows_ref):
    slots = bra_ref.shape[1]
    bra, ket = bra_ref[...], ket_ref[...]
    shell_a, shell_b = bra // 32, bra % 32
    shell_c, shell_d = ket // 32, ket % 32
    slot = lax.broadcasted_iota(jnp.int32, (1, slots), 1)
    live = slot < count_ref[0]
    klass = jnp.where(live, class_ref[...], SUBLANES - 1)
    factor = jnp.where(live, factor_ref[...], 0.0)

    def line(first, second):
        return (((first // 2) * 16 + second // 2) * 4 + (first % 2) * 2 + second % 2).astype(jnp.float32)

    fields = jnp.concatenate(
        (
            line(shell_c, shell_d),
            line(shell_a, shell_b),
            line(shell_b, shell_d),
            line(shell_a, shell_c),
            line(shell_b, shell_c),
            line(shell_a, shell_d),
            klass.astype(jnp.float32),
            factor,
        ),
        axis=0,
    )
    number = lax.broadcasted_iota(jnp.int32, (SUBLANES, slots), 0)
    same = jnp.where(klass == number, 1.0, 0.0)
    start = jnp.sum(jnp.where(klass < number, 1.0, 0.0), axis=1, keepdims=True)
    low = lax.broadcasted_iota(jnp.int32, (slots, slots), 0)
    high = lax.broadcasted_iota(jnp.int32, (slots, slots), 1)
    before = jnp.where(low < high, 1.0, 0.0).astype(jnp.bfloat16)
    rank = dot(same.astype(jnp.bfloat16), before, NN) + start
    rank = jnp.sum(rank * same, axis=0, keepdims=True).astype(jnp.int32)
    order = jnp.where(low == rank, 1.0, 0.0)
    rows_ref[...] = lax.dot_general(
        fields, order, NT, precision=lax.Precision.HIGHEST, preferred_element_type=jnp.float32
    )
    columns_ref[...] = lax.dot_general(
        order, fields, NT, precision=lax.Precision.HIGHEST, preferred_element_type=jnp.float32
    )


def sort_quartets(count, bra, ket, klass, factor):
    slots = bra.shape[1]
    vmem = pl.BlockSpec(memory_space=pltpu.VMEM)
    return pl.pallas_call(
        sort_kernel,
        out_shape=(
            jax.ShapeDtypeStruct((slots, SUBLANES), jnp.float32),
            jax.ShapeDtypeStruct((SUBLANES, slots), jnp.float32),
        ),
        in_specs=[pl.BlockSpec(memory_space=pltpu.SMEM)] + [vmem] * 4,
        out_specs=(vmem, vmem),
        name="sort_quartets",
    )(count, bra, ket, klass, factor)


STEP = 128


def quartet_kernel(
    ends_ref, blocks_ref, left_ref, right_ref, columns_ref, rows_ref, tables_ref,
    out_ref, scaled_ref, pieces_ref, totals_ref, found_ref, values_ref,
):
    classes = tables_ref.shape[0]
    pairs = pieces_ref.shape[0]
    width = totals_ref.shape[1]
    scaled_ref[...] = (blocks_ref[...].reshape(16, 16, SUBLANES, LANES) * left_ref[...][:, None]
                       * right_ref[...][None]).reshape(scaled_ref.shape)
    for half in range(2):
        high, low = split(scaled_ref[pl.ds(half, pairs, stride=2), :])
        pieces_ref[:, LANES * half:LANES * (half + 1)] = high
        pieces_ref[:, width + LANES * half:width + LANES * (half + 1)] = low
    totals_ref[...] = jnp.zeros_like(totals_ref)

    def step(index, carry):
        base = pl.multiple_of(index * STEP, STEP)
        here = pl.ds(base, STEP)
        columns = columns_ref[here, :]
        lane = lax.broadcasted_iota(jnp.int32, (STEP, pairs), 1)
        chosen = jnp.concatenate(
            [
                jnp.where(lane == columns[:, kind:kind + 1].astype(jnp.int32), 1.0, 0.0).astype(jnp.bfloat16)
                for kind in range(6)
            ],
            axis=0,
        )
        found_ref[...] = dot(chosen, pieces_ref[...], NN).astype(jnp.bfloat16)
        values_ref[...] = jnp.zeros_like(values_ref)
        for klass in range(classes):
            begin = 0 if klass == 0 else ends_ref[klass - 1]

            @pl.when((begin < base + STEP) & (ends_ref[klass] > base) & (begin < ends_ref[klass]))
            def _():
                factor = jnp.where(columns[:, 6:7] == klass, columns[:, 7:8], 0.0)
                for kind in range(6):
                    part = slice(STEP * kind, STEP * (kind + 1))
                    high, low = found_ref[part, :width], found_ref[part, width:]
                    form = kind // 2
                    dims = NT if kind % 2 == 0 else NN
                    product = dot(high, tables_ref[klass, form, 0], dims)
                    product += dot(high, tables_ref[klass, form, 1], dims)
                    product += dot(low, tables_ref[klass, form, 0], dims)
                    values_ref[part, :] += product * (factor if kind < 2 else -0.5 * factor)

        high, low = split(values_ref[...])
        sublane = lax.broadcasted_iota(jnp.int32, (pairs, STEP), 0)
        chosen = jnp.concatenate(
            [
                jnp.where(sublane == rows_ref[kind ^ 1:(kind ^ 1) + 1, here].astype(jnp.int32), 1.0, 0.0).astype(
                    jnp.bfloat16
                )
                for kind in range(6)
            ],
            axis=1,
        )
        totals_ref[...] += dot(chosen, high, NN) + dot(chosen, low, NN)
        return carry

    lax.fori_loop(0, (ends_ref[classes - 1] + STEP - 1) // STEP, step, 0)
    for half in range(2):
        scaled_ref[pl.ds(half, pairs, stride=2), :] = totals_ref[:, LANES * half:LANES * (half + 1)]
    out_ref[...] = (scaled_ref[...].reshape(16, 16, SUBLANES, LANES) * left_ref[...][:, None]
                    * right_ref[...][None]).reshape(out_ref.shape)


def add_quartets(ends, blocks, left, right, columns, rows, tables):
    lines = blocks.shape[0]
    width = tables.shape[-1]
    vmem = pl.BlockSpec(memory_space=pltpu.VMEM)
    return pl.pallas_call(
        quartet_kernel,
        out_shape=jax.ShapeDtypeStruct(blocks.shape, jnp.float32),
        in_specs=[pl.BlockSpec(memory_space=pltpu.SMEM)] + [vmem] * 6,
        out_specs=vmem,
        scratch_shapes=[
            pltpu.VMEM((lines, LANES), jnp.float32),
            pltpu.VMEM((lines // 2, 2 * width), jnp.bfloat16),
            pltpu.VMEM((lines // 2, width), jnp.float32),
            pltpu.VMEM((6 * STEP, 2 * width), jnp.bfloat16),
            pltpu.VMEM((6 * STEP, width), jnp.float32),
        ],
        compiler_params=pltpu.CompilerParams(vmem_limit_bytes=56 << 20),
        name="add_quartets",
    )(ends, blocks, left, right, columns, rows, tables)


def exchange(values):
    return lax.all_to_all(values, AXES, split_axis=0, concat_axis=0, tiled=True)


def on_device(
    density,
    core_hamiltonian,
    class_tables,
    shell_scale,
    block_place,
    work_blocks,
    quartet_bra,
    quartet_ket,
    quartet_class,
    quartet_factor,
    quartet_count,
):
    row_count = lax.axis_size("row")
    col_count = lax.axis_size("col")
    devices = row_count * col_count
    row_blocks = density.shape[0] // SHELL
    col_blocks = density.shape[1] // SHELL
    classes = class_tables.shape[0]
    own_tasks = work_blocks[0]
    places = block_place[own_tasks]
    row_part = (places % row_blocks * (2 * col_blocks)).reshape(row_count, 2)
    col_part = (places % col_blocks * 2).reshape(col_count, 2)
    outgoing = jnp.concatenate(
        (
            jnp.broadcast_to(row_part[:, None, :], (row_count, col_count, 2)),
            jnp.broadcast_to(col_part[None, :, :], (row_count, col_count, 2)),
        ),
        axis=2,
    )
    wanted = exchange(outgoing.reshape(devices, 4)).reshape(devices * 4)
    picked = pick_blocks(wanted, flatten_blocks(density), devices)
    blocks = exchange(picked.reshape(devices, SUBLANES, LANES))
    blocks = blocks.reshape(devices * SUBLANES, LANES)

    tables = make_tables(class_tables)
    scales = shell_scale.reshape(-1, SHELL)[own_tasks]
    left = jnp.broadcast_to(
        scales.reshape(row_count, 2, 1, 2, SUBLANES, 1), (row_count, 2, 2, 2, SUBLANES, SHELL)
    ).reshape(row_count, SUBLANES, LANES)
    right = jnp.broadcast_to(
        scales.reshape(col_count, 1, 2, 1, 1, SHELL), (col_count, 2, 2, 2, SUBLANES, SHELL)
    ).reshape(col_count, SUBLANES, LANES)
    columns, rows = sort_quartets(quartet_count, quartet_bra, quartet_ket, quartet_class, quartet_factor)
    slots = quartet_class.shape[1]
    within = jnp.where(jnp.arange(slots) < quartet_count[0], quartet_class[0], classes)
    ends = jnp.sum((within[None, :] <= jnp.arange(classes)[:, None]).astype(jnp.int32), axis=1)
    summed = add_quartets(ends, blocks, left, right, columns, rows, tables)
    returned = exchange(summed.reshape(devices, SUBLANES, LANES))
    return merge_blocks(wanted, returned.reshape(devices * SUBLANES, LANES), core_hamiltonian)


def solution(mesh):
    placed = (
        P("row", "col"),
        P("row", "col"),
        P(),
        P(),
        P(),
        P(("row", "col"), None),
        P(("row", "col"), None),
        P(("row", "col"), None),
        P(("row", "col"), None),
        P(("row", "col"), None),
        P(("row", "col")),
    )
    return jax.shard_map(
        on_device, mesh=mesh, in_specs=placed, out_specs=P("row", "col"), check_vma=False
    )
```

time: 175 us -> 136 us (0.78)
  blocking collectives: 91.1 us -> 45 us
  Pallas kernels: 65.2 us -> 32 us
  waiting for transfers between devices: 0.01 us -> 26.1 us
  starting transfers between devices: 5.6 us -> 21.2 us
    all_to_all x2 -> x1, blocking collectives: 91.1 us -> 45 us  [exchange(): return lax.all_to_all(values, AXES, split_axis=0, concat_axis=0, tiled=True)]
    all_to_all x1 -> x2, waiting for transfers between devices: 0.01 us -> 26.1 us  [exchange(): return lax.all_to_all(values, AXES, split_axis=0, concat_axis=0, tiled=True)]
    pallas_call x1, Pallas kernels: 29.4 us -> 6.43 us  [make_tables(): pl.pallas_call(table_kernel, grid=(classes,), out_shape=jax.ShapeDtypeStr...]
    all_to_all x1 -> x2, starting transfers between devices: 5.6 us -> 21.2 us  [exchange(): return lax.all_to_all(values, AXES, split_axis=0, concat_axis=0, tiled=True)]
    pallas_call x1, Pallas kernels: 13.1 us -> 3.92 us  [pick_blocks(): pl.pallas_call(pick_kernel, out_shape=jax.ShapeDtypeStruct((devices * SUB...]
    pallas_call x1, Pallas kernels: 13.3 us -> 5.19 us  [merge_blocks(): pl.pallas_call(merge_kernel, out_shape=jax.ShapeDtypeStruct(core.shape, j...]
    pallas_call x0 -> x2, Pallas kernels: none -> 7.63 us  [the longest x1 4.15 us: flatten_blocks(): pl.pallas_call(flatten_kernel, out_shape=jax.ShapeDtypeStruct((2 * blocks...]
    unnamed x24 -> x16, local copies, waits for them, and re-layouts: 4.07 us -> 2.63 us
  transfers between devices with their start and end apart: 1 -> 2, of which waited for: 0 -> 2; matrix products, arithmetic and copies ran while one was open for 3% -> 2% of each run, Pallas kernels for 17% -> 10%
where the time goes in v2:
time: 136 us
  blocking collectives  45 us (33%)
  Pallas kernels  32 us (24%)
  waiting for transfers between devices  26.1 us (19%)
  starting transfers between devices  21.2 us (16%)
  local copies, waits for them, and re-layouts  8.25 us (6%)
  other arithmetic  2.35 us (2%)
    all_to_all x1, blocking collectives, exchange(): return lax.all_to_all(values, AXES, split_axis=0, concat_axis=0, tiled=True)  45 us
    all_to_all x2, waiting for transfers between devices, exchange(): return lax.all_to_all(values, AXES, split_axis=0, concat_axis=0, tiled=True)  26.1 us
    all_to_all x2, starting transfers between devices, exchange(): return lax.all_to_all(values, AXES, split_axis=0, concat_axis=0, tiled=True)  21.2 us
    pallas_call x1, Pallas kernels, add_quartets(): pl.pallas_call(quartet_kernel, out_shape=jax.ShapeDtypeStruct(blocks.shap...  8.79 us
    pallas_call x1, Pallas kernels, make_tables(): pl.pallas_call(table_kernel, grid=(classes,), out_shape=jax.ShapeDtypeStr...  6.43 us
    pallas_call x1, Pallas kernels, merge_blocks(): pl.pallas_call(merge_kernel, out_shape=jax.ShapeDtypeStruct(core.shape, j...  5.19 us
    pallas_call x1, Pallas kernels, flatten_blocks(): pl.pallas_call(flatten_kernel, out_shape=jax.ShapeDtypeStruct((2 * blocks...  4.15 us
    pallas_call x1, Pallas kernels, pick_blocks(): pl.pallas_call(pick_kernel, out_shape=jax.ShapeDtypeStruct((devices * SUB...  3.92 us
  transfers between devices with their start and end apart: 2, of which 2 were waited for; matrix products, arithmetic and copies ran while one was open for 2% of the time, Pallas kernels for 10%

profile of v2, /device:TPU:1, one launch (start us, length us, event | category | flops | bytes accessed | tf_op | source)
XLA Modules:
  0.0 135.7 jit_solution(7135081171612459877)
XLA Ops:
  0.0 0.7 fusion
  0.7 0.0 copy-done
  0.7 0.7 gather_fusion
  1.4 0.1 rem.25
  1.5 0.1 copy.18
  1.6 0.1 broadcast_in_dim.16
  1.7 0.8 copy.22
  2.5 15.7 %all-to-all-start = ((s32[256,1,4]{2,1,0:T(1,128)}), s32[256,1,4]{2,1,0:T(1,128)S(1)}, u32[]{:S(2)}, u32[]{:S(2)}) async-start(s32[256,1,4]{2,1,0:T(1,128)} %bitcast.2), calls=%async_computation | async-start | bytes 262144 | tf_op jit(solution)/shard_map/all_to_all | solution.py:347
  18.1 4.1 %flatten_blocks.1.flat_ref = f32[3200,128]{1,0:T(8,128)} custom-call(f32[640,640]{1,0:T(8,128)} %density_ref.1), custom_call_target="tpu_custom_call" | custom-call | tf_op jit(solution)/shard_map/flatten_blocks/pallas_call | solution.py:57
  22.3 9.0 %all-to-all-done = s32[256,1,4]{2,1,0:T(1,128)S(1)} async-done(((s32[256,1,4]{2,1,0:T(1,128)}), s32[256,1,4]{2,1,0:T(1,128)S(1)}, u32[]{:S(2)}, u32[]{:S(2)}) %all-to-all-start) | async-done | bytes 4128 | tf_op jit(solution)/shard_map/all_to_all | solution.py:347
  31.3 0.6 broadcast.94
  31.9 1.0 reduce.3
  32.9 0.7 reshape.92.wanted_ref
  33.6 3.9 %pick_blocks.1 = f32[2048,128]{1,0:T(8,128)} custom-call(s32[1024]{0:T(1024)} %reshape.92.wanted_ref, f32[3200,128]{1,0:T(8,128)} %flatten_blocks.1.flat_ref), custom_call_target="tpu_custom_call" | custom-call | tf_op jit(solution)/shard_map/pick_blocks/pallas_call | solution.py:76
  37.5 5.6 %all-to-all-start.1 = ((f32[256,8,128]{2,1,0:T(8,128)}), f32[256,8,128]{2,1,0:T(8,128)S(1)}, u32[]{:S(2)}, u32[]{:S(2)}) async-start(f32[256,8,128]{2,1,0:T(8,128)} %bitcast.18), calls=%async_computation.1 | async-start | bytes 2097152 | tf_op jit(solution)/shard_map/all_to_all | solution.py:347
  43.1 0.0 copy-start.3
  43.8 0.1 reshape.95
  44.0 0.6 gather_fusion.1
  44.5 0.1 broadcast_in_dim.35
  44.6 0.1 broadcast_in_dim.36
  44.8 0.8 reshape.96.left_ref
  45.6 0.8 reshape.97.right_ref
  46.5 6.4 %make_tables.1.tables_ref = bf16[4,3,2,256,256]{4,3,2,1,0:T(8,128)(2,1)S(1)} custom-call(f32[4,256,256]{2,1,0:T(8,128)S(1)} %copy-done.3), custom_call_target="tpu_custom_call" | custom-call | tf_op jit(solution)/shard_map/make_tables/pallas_call | solution.py:182
  52.9 1.6 %copy-done.1 = bf16[4,3,2,256,256]{4,3,2,1,0:T(8,128)(2,1)} copy-done((bf16[4,3,2,256,256]{4,3,2,1,0:T(8,128)(2,1)}, bf16[4,3,2,256,256]{4,3,2,1,0:T(8,128)(2,1)S(1)}, u32[]{:S(2)}) %copy-start.1) | copy-done | bytes 3145752
  54.5 3.5 %sort_quartets.1 = (f32[512,8]{1,0:T(8,128)}, f32[8,512]{1,0:T(8,128)}) custom-call(s32[1]{0:T(128)} %copy.23.count_ref, s32[1,512]{1,0:T(1,128)} %bra_ref.1, s32[1,512]{1,0:T(1,128)} %ket_ref.1, s32[1,512]{1,0:T(1,128)} %class_ref.1, f32[1,512]{1,0:T(1,128)} %factor_ref.1), custom_call_target="tpu_custom_call" | custom-call | tf_op jit(solution)/shard_map/sort_quartets/pallas_call | solution.py:244
  58.0 0.0 copy-done.7
  58.0 0.6 convert_reduce_fusion.ends_ref
  58.7 17.1 %all-to-all-done.1 = f32[256,8,128]{2,1,0:T(8,128)S(1)} async-done(((f32[256,8,128]{2,1,0:T(8,128)}), f32[256,8,128]{2,1,0:T(8,128)S(1)}, u32[]{:S(2)}, u32[]{:S(2)}) %all-to-all-start.1) | async-done | bytes 1048608 | tf_op jit(solution)/shard_map/all_to_all | solution.py:347
  75.7 1.0 copy-done.5
  76.7 8.8 %add_quartets.1 = f32[2048,128]{1,0:T(8,128)} custom-call(s32[4]{0:T(128)} %convert_reduce_fusion.ends_ref, f32[2048,128]{1,0:T(8,128)} %bitcast.19, f32[16,8,128]{2,1,0:T(8,128)} %reshape.96.left_ref, f32[16,8,128]{2,1,0:T(8,128)} %reshape.97.right_ref, f32[512,8]{1,0:T(8,128)} %get-tuple-element.7.columns_ref, f32[8,512]{1,0:T(8,128)} %get-tuple-element.8.rows_ref, ...), custom_call_target="tpu_custom_call" | custom-call | tf_op jit(solution)/shard_map/add_quartets/pallas_call | solution.py:329
  85.5 45.0 %all_to_all.19 = f32[256,8,128]{2,1,0:T(8,128)S(1)} all-to-all(f32[256,8,128]{2,1,0:T(8,128)} %bitcast.20), channel_id=1, replica_groups=mesh['row'=16,'col'=16] {'row','col'}, dimensions={0} | all-to-all | bytes 2097152 | tf_op jit(solution)/shard_map/all_to_all | solution.py:347
  130.5 5.2 %merge_blocks.1 = f32[640,640]{1,0:T(8,128)} custom-call(s32[1024]{0:T(1024)S(1)} %copy-done.4, f32[2048,128]{1,0:T(8,128)S(1)} %bitcast.17, f32[640,640]{1,0:T(8,128)S(1)} %copy-done.2), custom_call_target="tpu_custom_call" | custom-call | tf_op jit(solution)/shard_map/merge_blocks/pallas_call | solution.py:124
  (18 shorter events, 0.1 us)
Async XLA Ops:
  0.0 0.7 copy-start
  2.5 28.8 %all-to-all-start = ((s32[256,1,4]{2,1,0:T(1,128)}), s32[256,1,4]{2,1,0:T(1,128)S(1)}, u32[]{:S(2)}, u32[]{:S(2)}) async-start(s32[256,1,4]{2,1,0:T(1,128)} %bitcast.2), calls=%async_computation | async-start | bytes 262144 | tf_op jit(solution)/shard_map/all_to_all | solution.py:347
  37.5 6.3 %copy-start.6 = (f32[10240]{0:T(1024)S(1)}, f32[10240]{0:T(1024)}, u32[]{:S(2)}) copy-start(f32[10240]{0:T(1024)} %param.14) | copy-start | bytes 122884
  37.5 38.2 %all-to-all-start.1 = ((f32[256,8,128]{2,1,0:T(8,128)}), f32[256,8,128]{2,1,0:T(8,128)S(1)}, u32[]{:S(2)}, u32[]{:S(2)}) async-start(f32[256,8,128]{2,1,0:T(8,128)} %bitcast.18), calls=%async_computation.1 | async-start | bytes 2097152 | tf_op jit(solution)/shard_map/all_to_all | solution.py:347
  43.1 3.4 %copy-start.3 = (f32[4,256,256]{2,1,0:T(8,128)S(1)}, f32[4,256,256]{2,1,0:T(8,128)}, u32[]{:S(2)}) copy-start(f32[4,256,256]{2,1,0:T(8,128)} %tables_ref.1) | copy-start | bytes 3145732
  46.5 11.6 %copy-start.7 = (s32[1,512]{1,0:T(1,128)S(1)}, s32[1,512]{1,0:T(1,128)}, u32[]{:S(2)}) copy-start(s32[1,512]{1,0:T(1,128)} %class_ref.1) | copy-start | bytes 6148
  52.9 1.6 %copy-start.1 = (bf16[4,3,2,256,256]{4,3,2,1,0:T(8,128)(2,1)}, bf16[4,3,2,256,256]{4,3,2,1,0:T(8,128)(2,1)S(1)}, u32[]{:S(2)}) copy-start(bf16[4,3,2,256,256]{4,3,2,1,0:T(8,128)(2,1)S(1)} %make_tables.1.tables_ref) | copy-start | bytes 9437188
  75.7 1.0 copy-start.5
  85.5 45.0 %copy-start.2 = (f32[640,640]{1,0:T(8,128)S(1)}, f32[640,640]{1,0:T(8,128)}, u32[]{:S(2)}) copy-start(f32[640,640]{1,0:T(8,128)} %core_ref.1) | copy-start | bytes 4915204
  85.5 45.0 %copy-start.4 = (s32[1024]{0:T(1024)S(1)}, s32[1024]{0:T(1024)}, u32[]{:S(2)}) copy-start(s32[1024]{0:T(1024)} %reshape.92.wanted_ref) | copy-start | bytes 12292

commit v3 on v2

--- a/solution.py
+++ b/solution.py
@@ -10,6 +10,7 @@
 SHELL = 16
 LANES = 128
 SUBLANES = 8
+VMEM_BYTES = 16 << 20
 GROUPS = LANES // SHELL
 AXES = ("row", "col")
 NT = (((1,), (1,)), ((), ()))
@@ -57,6 +58,7 @@
     return pl.pallas_call(
         flatten_kernel,
         out_shape=jax.ShapeDtypeStruct((2 * blocks, LANES), jnp.float32),
+        compiler_params=pltpu.CompilerParams(vmem_limit_bytes=VMEM_BYTES),
         name="flatten_blocks",
     )(density)
 
@@ -64,7 +66,7 @@
 def pick_kernel(wanted_ref, flat_ref, out_ref):
     def pick(device, carry):
         for part in range(4):
-            source = pl.multiple_of(wanted_ref[4 * device + part // 2] + wanted_ref[4 * device + 2 + part % 2], 2)
+            source = pl.multiple_of(wanted_ref[device, 0, part // 2] + wanted_ref[device, 0, 2 + part % 2], 2)
             target = pl.multiple_of(SUBLANES * device + 2 * part, 2)
             out_ref[pl.ds(target, 2), :] = flat_ref[pl.ds(source, 2), :]
         return carry
@@ -81,6 +83,7 @@
             pl.BlockSpec(memory_space=pltpu.VMEM),
         ],
         out_specs=pl.BlockSpec(memory_space=pltpu.VMEM),
+        compiler_params=pltpu.CompilerParams(vmem_limit_bytes=VMEM_BYTES),
         name="pick_blocks",
     )(wanted, flat)
 
@@ -95,7 +98,7 @@
         places = []
         sums = []
         for part in range(4):
-            place = wanted_ref[4 * device + part // 2] + wanted_ref[4 * device + 2 + part % 2]
+            place = wanted_ref[device, 0, part // 2] + wanted_ref[device, 0, 2 + part % 2]
             place = pl.ds(pl.multiple_of(place, 2), 2)
             source = pl.multiple_of(SUBLANES * device + 2 * part, 2)
             places.append(place)
@@ -131,18 +134,19 @@
         ],
         out_specs=pl.BlockSpec(memory_space=pltpu.VMEM),
         scratch_shapes=[pltpu.VMEM((2 * blocks, LANES), jnp.float32)],
-        compiler_params=pltpu.CompilerParams(vmem_limit_bytes=40 << 20),
+        compiler_params=pltpu.CompilerParams(vmem_limit_bytes=VMEM_BYTES),
         name="merge_blocks",
     )(wanted, parts, core)
 
 
 def table_kernel(tables_ref, out_ref, mid_ref, turned_ref, last_ref):
-    table = tables_ref[0]
-    width = table.shape[0]
+    width = tables_ref.shape[1]
     halves = range(2)
-    high, low = split(table)
-    out_ref[0, 0, 0] = high
-    out_ref[0, 0, 1] = low
+
+    def keep(form, values):
+        out_ref[0, form, 0], out_ref[0, form, 1] = split(values)
+
+    keep(0, tables_ref[0])
 
     def swap_inner(first, carry):
         for a in halves:
@@ -154,10 +158,8 @@
         return carry
 
     lax.fori_loop(0, width // SHELL, swap_inner, 0, unroll=4)
-    high, low = split(mid_ref[...])
-    out_ref[0, 1, 0] = high
-    out_ref[0, 1, 1] = low
     turned = mid_ref[...].T
+    keep(1, mid_ref[...])
     for b in halves:
         turned_ref[b] = turned[:, LANES * b:LANES * (b + 1)]
 
@@ -171,10 +173,8 @@
         return carry
 
     lax.fori_loop(0, SHELL, swap_outer, 0, unroll=4)
-    for a in halves:
-        high, low = split(last_ref[a])
-        out_ref[0, 2, 0, :, LANES * a:LANES * (a + 1)] = high
-        out_ref[0, 2, 1, :, LANES * a:LANES * (a + 1)] = low
+    last = jnp.concatenate((last_ref[0], last_ref[1]), axis=1)
+    keep(2, last)
 
 
 def make_tables(class_tables):
@@ -190,7 +190,7 @@
             pltpu.VMEM((2, width, LANES), jnp.float32),
             pltpu.VMEM((2, width, LANES), jnp.float32),
         ],
-        compiler_params=pltpu.CompilerParams(vmem_limit_bytes=40 << 20),
+        compiler_params=pltpu.CompilerParams(vmem_limit_bytes=VMEM_BYTES),
         name="make_tables",
     )(class_tables)
 
@@ -249,6 +249,7 @@
         ),
         in_specs=[pl.BlockSpec(memory_space=pltpu.SMEM)] + [vmem] * 4,
         out_specs=(vmem, vmem),
+        compiler_params=pltpu.CompilerParams(vmem_limit_bytes=VMEM_BYTES),
         name="sort_quartets",
     )(count, bra, ket, klass, factor)
 
@@ -283,7 +284,11 @@
             ],
             axis=0,
         )
-        found_ref[...] = dot(chosen, pieces_ref[...], NN).astype(jnp.bfloat16)
+        found = dot(chosen, pieces_ref[...], NN).astype(jnp.bfloat16)
+        for kind in range(6):
+            part = slice(STEP * kind, STEP * (kind + 1))
+            found_ref[kind, :STEP] = found[part, :width]
+            found_ref[kind, STEP:] = found[part, width:]
         values_ref[...] = jnp.zeros_like(values_ref)
         for klass in range(classes):
             begin = 0 if klass == 0 else ends_ref[klass - 1]
@@ -293,12 +298,10 @@
                 factor = jnp.where(columns[:, 6:7] == klass, columns[:, 7:8], 0.0)
                 for kind in range(6):
                     part = slice(STEP * kind, STEP * (kind + 1))
-                    high, low = found_ref[part, :width], found_ref[part, width:]
-                    form = kind // 2
                     dims = NT if kind % 2 == 0 else NN
-                    product = dot(high, tables_ref[klass, form, 0], dims)
-                    product += dot(high, tables_ref[klass, form, 1], dims)
-                    product += dot(low, tables_ref[klass, form, 0], dims)
+                    product = dot(found_ref[kind], tables_ref[klass, kind // 2, 0], dims)
+                    product = product[:STEP] + product[STEP:]
+                    product += dot(found_ref[kind, :STEP], tables_ref[klass, kind // 2, 1], dims)
                     values_ref[part, :] += product * (factor if kind < 2 else -0.5 * factor)
 
         high, low = split(values_ref[...])
@@ -335,10 +338,10 @@
             pltpu.VMEM((lines, LANES), jnp.float32),
             pltpu.VMEM((lines // 2, 2 * width), jnp.bfloat16),
             pltpu.VMEM((lines // 2, width), jnp.float32),
-            pltpu.VMEM((6 * STEP, 2 * width), jnp.bfloat16),
+            pltpu.VMEM((6, 2 * STEP, width), jnp.bfloat16),
             pltpu.VMEM((6 * STEP, width), jnp.float32),
         ],
-        compiler_params=pltpu.CompilerParams(vmem_limit_bytes=56 << 20),
+        compiler_params=pltpu.CompilerParams(vmem_limit_bytes=VMEM_BYTES),
         name="add_quartets",
     )(ends, blocks, left, right, columns, rows, tables)
 
@@ -377,7 +380,7 @@
         ),
         axis=2,
     )
-    wanted = exchange(outgoing.reshape(devices, 4)).reshape(devices * 4)
+    wanted = exchange(outgoing.reshape(devices, 1, 4))
     picked = pick_blocks(wanted, flatten_blocks(density), devices)
     blocks = exchange(picked.reshape(devices, SUBLANES, LANES))
     blocks = blocks.reshape(devices * SUBLANES, LANES)

time: 136 us -> 135 us (level)
  Pallas kernels: 32 us -> 28.6 us
  waiting for transfers between devices: 26.1 us -> 29.3 us
  starting transfers between devices: 21.2 us -> 22.8 us
  other arithmetic: 2.35 us -> 0.85 us
    all_to_all x2, waiting for transfers between devices: 26.1 us -> 29.3 us  [exchange(): return lax.all_to_all(values, AXES, split_axis=0, concat_axis=0, tiled=True)]
    pallas_call x1, Pallas kernels: 8.79 us -> 6.14 us  [add_quartets(): pl.pallas_call(quartet_kernel, out_shape=jax.ShapeDtypeStruct(blocks.shap...]
    pallas_call x1, Pallas kernels: 4.15 us -> 1.55 us  [flatten_blocks(): pl.pallas_call(flatten_kernel, out_shape=jax.ShapeDtypeStruct((2 * blocks...]
    pallas_call x1, Pallas kernels: 5.19 us -> 7.28 us  [merge_blocks(): pl.pallas_call(merge_kernel, out_shape=jax.ShapeDtypeStruct(core.shape, j...]
    unnamed x16 -> x22, local copies, waits for them, and re-layouts: 2.63 us -> 4.34 us
    all_to_all x2, starting transfers between devices: 21.2 us -> 22.8 us  [exchange(): return lax.all_to_all(values, AXES, split_axis=0, concat_axis=0, tiled=True)]
    pallas_call x1, Pallas kernels: 3.49 us -> 2.06 us  [sort_quartets(): pl.pallas_call(sort_kernel, out_shape=(jax.ShapeDtypeStruct((slots, SUBLA...]
  transfers between devices with their start and end apart: 2 -> 2, of which waited for: 2 -> 2; matrix products, arithmetic and copies ran while one was open for 2% -> 1% of each run, Pallas kernels for 10% -> 7%
where the time goes in v3:
time: 135 us; the launch traced here: 134 us
  blocking collectives  44.7 us (33%)
  waiting for transfers between devices  29.3 us (22%)
  Pallas kernels  28.6 us (21%)
  starting transfers between devices  22.8 us (17%)
  local copies, waits for them, and re-layouts  7.43 us (6%)
    all_to_all x1, blocking collectives, exchange(): return lax.all_to_all(values, AXES, split_axis=0, concat_axis=0, tiled=True)  44.7 us
    all_to_all x2, waiting for transfers between devices, exchange(): return lax.all_to_all(values, AXES, split_axis=0, concat_axis=0, tiled=True)  29.3 us
    all_to_all x2, starting transfers between devices, exchange(): return lax.all_to_all(values, AXES, split_axis=0, concat_axis=0, tiled=True)  22.8 us
    pallas_call x1, Pallas kernels, merge_blocks(): pl.pallas_call(merge_kernel, out_shape=jax.ShapeDtypeStruct(core.shape, j...  7.28 us
    pallas_call x1, Pallas kernels, make_tables(): pl.pallas_call(table_kernel, grid=(classes,), out_shape=jax.ShapeDtypeStr...  6.38 us
    pallas_call x1, Pallas kernels, add_quartets(): pl.pallas_call(quartet_kernel, out_shape=jax.ShapeDtypeStruct(blocks.shap...  6.14 us
    pallas_call x1, Pallas kernels, pick_blocks(): pl.pallas_call(pick_kernel, out_shape=jax.ShapeDtypeStruct((devices * SUB...  5.16 us
    unnamed x22, local copies, waits for them, and re-layouts  4.34 us
  transfers between devices with their start and end apart: 2, of which 2 were waited for; matrix products, arithmetic and copies ran while one was open for 1% of the time, Pallas kernels for 7%

profile of v3, /device:TPU:1, one launch (start us, length us, event | category | flops | bytes accessed | tf_op | source)
XLA Modules:
  0.0 134.4 jit_solution(7736051612029301340)
XLA Ops:
  0.0 0.7 fusion
  0.7 0.0 copy-done
  0.7 0.7 gather_fusion
  1.4 0.1 rem.25
  1.5 0.1 copy.18
  1.6 0.1 broadcast_in_dim.16
  1.7 0.8 copy.22
  2.5 15.7 %all-to-all-start = ((s32[256,1,4]{2,1,0:T(1,128)}), s32[256,1,4]{2,1,0:T(1,128)S(1)}, u32[]{:S(2)}, u32[]{:S(2)}) async-start(s32[256,1,4]{2,1,0:T(1,128)} %bitcast.2), calls=%async_computation | async-start | bytes 262144 | tf_op jit(solution)/shard_map/all_to_all | solution.py:350
  18.1 0.0 copy-start.1
  18.2 1.4 %copy-done.1 = f32[640,640]{1,0:T(8,128)S(1)} copy-done((f32[640,640]{1,0:T(8,128)S(1)}, f32[640,640]{1,0:T(8,128)}, u32[]{:S(2)}) %copy-start.1) | copy-done | bytes 1638424
  19.6 1.5 %flatten_blocks.1.flat_ref = f32[3200,128]{1,0:T(8,128)S(1)} custom-call(f32[640,640]{1,0:T(8,128)S(1)} %copy-done.1), custom_call_target="tpu_custom_call" | custom-call | tf_op jit(solution)/shard_map/flatten_blocks/pallas_call | solution.py:58
  21.1 10.1 %all-to-all-done.wanted_ref = s32[256,1,4]{2,1,0:T(1,128)S(1)} async-done(((s32[256,1,4]{2,1,0:T(1,128)}), s32[256,1,4]{2,1,0:T(1,128)S(1)}, u32[]{:S(2)}, u32[]{:S(2)}) %all-to-all-start) | async-done | bytes 4128 | tf_op jit(solution)/shard_map/all_to_all | solution.py:350
  31.2 5.2 %pick_blocks.1 = f32[2048,128]{1,0:T(8,128)} custom-call(s32[256,1,4]{2,1,0:T(1,128)S(1)} %all-to-all-done.wanted_ref, f32[3200,128]{1,0:T(8,128)S(1)} %flatten_blocks.1.flat_ref), custom_call_target="tpu_custom_call" | custom-call | tf_op jit(solution)/shard_map/pick_blocks/pallas_call | solution.py:78
  36.4 7.2 %all-to-all-start.1 = ((f32[256,8,128]{2,1,0:T(8,128)}), f32[256,8,128]{2,1,0:T(8,128)}, u32[]{:S(2)}, u32[]{:S(2)}) async-start(f32[256,8,128]{2,1,0:T(8,128)} %bitcast.5), calls=%async_computation.1 | async-start | bytes 2097152 | tf_op jit(solution)/shard_map/all_to_all | solution.py:350
  44.2 0.1 reshape.90
  44.4 0.6 gather_fusion.1
  45.0 0.1 broadcast_in_dim.35
  45.1 0.1 broadcast_in_dim.36
  45.2 0.2 reshape.91.left_ref
  45.4 0.2 reshape.92.right_ref
  45.6 0.0 copy-start.3
  45.6 1.2 copy-done.3
  46.9 6.4 %make_tables.1.tables_ref = bf16[4,3,2,256,256]{4,3,2,1,0:T(8,128)(2,1)S(1)} custom-call(f32[4,256,256]{2,1,0:T(8,128)S(1)} %copy-done.3), custom_call_target="tpu_custom_call" | custom-call | tf_op jit(solution)/shard_map/make_tables/pallas_call | solution.py:182
  53.3 2.1 %sort_quartets.1 = (f32[512,8]{1,0:T(8,128)S(1)}, f32[8,512]{1,0:T(8,128)S(1)}) custom-call(s32[1]{0:T(128)} %copy.23.count_ref, s32[1,512]{1,0:T(1,128)S(1)} %copy-done.7, s32[1,512]{1,0:T(1,128)S(1)} %copy-done.8, s32[1,512]{1,0:T(1,128)S(1)} %copy-done.6, f32[1,512]{1,0:T(1,128)S(1)} %copy-done.9), custom_call_target="tpu_custom_call" | custom-call | tf_op jit(solution)/shard_map/sort_quartets/pallas_call | solution.py:244
  55.4 0.7 copy-done.4
  56.1 0.1 convert_reduce_fusion.ends_ref
  56.2 19.2 %all-to-all-done.1 = f32[256,8,128]{2,1,0:T(8,128)} async-done(((f32[256,8,128]{2,1,0:T(8,128)}), f32[256,8,128]{2,1,0:T(8,128)}, u32[]{:S(2)}, u32[]{:S(2)}) %all-to-all-start.1) | async-done | bytes 1048608 | tf_op jit(solution)/shard_map/all_to_all | solution.py:350
  75.4 0.9 copy-done.5
  76.3 6.1 %add_quartets.1 = f32[2048,128]{1,0:T(8,128)S(1)} custom-call(s32[4]{0:T(128)S(1)} %convert_reduce_fusion.ends_ref, f32[2048,128]{1,0:T(8,128)} %bitcast.6.blocks_ref, f32[16,8,128]{2,1,0:T(8,128)S(1)} %reshape.91.left_ref, f32[16,8,128]{2,1,0:T(8,128)S(1)} %reshape.92.right_ref, f32[512,8]{1,0:T(8,128)S(1)} %copy-done.5, ...), custom_call_target="tpu_custom_call" | custom-call | tf_op jit(solution)/shard_map/add_quartets/pallas_call | solution.py:332
  82.5 0.0 copy-start.2
  82.5 44.7 %all_to_all.15 = f32[256,8,128]{2,1,0:T(8,128)S(1)} all-to-all(f32[256,8,128]{2,1,0:T(8,128)S(1)} %bitcast.18), channel_id=1, replica_groups=mesh['row'=16,'col'=16] {'row','col'}, dimensions={0} | all-to-all | bytes 2097152 | tf_op jit(solution)/shard_map/all_to_all | solution.py:350
  127.2 7.3 %merge_blocks.1 = f32[640,640]{1,0:T(8,128)} custom-call(s32[256,1,4]{2,1,0:T(1,128)S(1)} %all-to-all-done.wanted_ref, f32[2048,128]{1,0:T(8,128)S(1)} %bitcast.17, f32[640,640]{1,0:T(8,128)S(1)} %copy-done.2), custom_call_target="tpu_custom_call" | custom-call | tf_op jit(solution)/shard_map/merge_blocks/pallas_call | solution.py:127
  (21 shorter events, 0.1 us)
Async XLA Ops:
  0.0 0.7 copy-start
  2.5 28.7 %all-to-all-start = ((s32[256,1,4]{2,1,0:T(1,128)}), s32[256,1,4]{2,1,0:T(1,128)S(1)}, u32[]{:S(2)}, u32[]{:S(2)}) async-start(s32[256,1,4]{2,1,0:T(1,128)} %bitcast.2), calls=%async_computation | async-start | bytes 262144 | tf_op jit(solution)/shard_map/all_to_all | solution.py:350
  18.1 1.4 %copy-start.1 = (f32[640,640]{1,0:T(8,128)S(1)}, f32[640,640]{1,0:T(8,128)}, u32[]{:S(2)}) copy-start(f32[640,640]{1,0:T(8,128)} %density_ref.1) | copy-start | bytes 4915204
  36.4 7.8 %copy-start.10 = (f32[10240]{0:T(1024)S(1)}, f32[10240]{0:T(1024)}, u32[]{:S(2)}) copy-start(f32[10240]{0:T(1024)} %param.14) | copy-start | bytes 122884
  36.4 39.0 %all-to-all-start.1 = ((f32[256,8,128]{2,1,0:T(8,128)}), f32[256,8,128]{2,1,0:T(8,128)}, u32[]{:S(2)}, u32[]{:S(2)}) async-start(f32[256,8,128]{2,1,0:T(8,128)} %bitcast.5), calls=%async_computation.1 | async-start | bytes 2097152 | tf_op jit(solution)/shard_map/all_to_all | solution.py:350
  45.6 1.2 copy-start.3
  46.9 6.4 %copy-start.6 = (s32[1,512]{1,0:T(1,128)S(1)}, s32[1,512]{1,0:T(1,128)}, u32[]{:S(2)}) copy-start(s32[1,512]{1,0:T(1,128)} %class_ref.1) | copy-start | bytes 6148
  46.9 6.4 %copy-start.7 = (s32[1,512]{1,0:T(1,128)S(1)}, s32[1,512]{1,0:T(1,128)}, u32[]{:S(2)}) copy-start(s32[1,512]{1,0:T(1,128)} %bra_ref.1) | copy-start | bytes 6148
  46.9 6.4 %copy-start.8 = (s32[1,512]{1,0:T(1,128)S(1)}, s32[1,512]{1,0:T(1,128)}, u32[]{:S(2)}) copy-start(s32[1,512]{1,0:T(1,128)} %ket_ref.1) | copy-start | bytes 6148
  46.9 6.4 %copy-start.9 = (f32[1,512]{1,0:T(1,128)S(1)}, f32[1,512]{1,0:T(1,128)}, u32[]{:S(2)}) copy-start(f32[1,512]{1,0:T(1,128)} %factor_ref.1) | copy-start | bytes 6148
  55.4 0.7 copy-start.4
  75.4 1.0 copy-start.5
  82.5 44.7 %copy-start.2 = (f32[640,640]{1,0:T(8,128)S(1)}, f32[640,640]{1,0:T(8,128)}, u32[]{:S(2)}) copy-start(f32[640,640]{1,0:T(8,128)} %core_ref.1) | copy-start | bytes 4915204

commit v4 on v3

--- a/solution.py
+++ b/solution.py
@@ -10,6 +10,7 @@
 SHELL = 16
 LANES = 128
 SUBLANES = 8
+STRIPE = 40
 VMEM_BYTES = 16 << 20
 GROUPS = LANES // SHELL
 AXES = ("row", "col")
@@ -34,6 +35,45 @@
 
 def dot(left, right, dims):
     return lax.dot_general(left, right, dims, preferred_element_type=jnp.float32)
+
+
+def ask_kernel(work_ref, place_ref, out_ref):
+    tasks = work_ref.shape[1]
+    devices = out_ref.shape[0]
+    row = lax.broadcasted_iota(jnp.int32, (tasks, tasks), 0)
+    lane = lax.broadcasted_iota(jnp.int32, (tasks, tasks), 1)
+    work = jnp.sum(jnp.where(row == lane, work_ref[...], 0).astype(jnp.float32), axis=1, keepdims=True)
+    work = work.astype(jnp.int32)
+    lane = lax.broadcasted_iota(jnp.int32, (tasks, LANES), 1)
+    table = jnp.zeros((tasks, LANES), jnp.float32)
+    for part in range(place_ref.shape[0]):
+        hit = work == lane + part * LANES
+        table += jnp.where(hit, place_ref[part:part + 1, :], 0).astype(jnp.float32)
+    place = jnp.sum(table, axis=1, keepdims=True).astype(jnp.int32) % STRIPE
+    first = (place * (2 * STRIPE)).astype(jnp.float32)
+    second = (place * 2).astype(jnp.float32)
+    values = jnp.concatenate((first, first, second, second), axis=0)
+    row = lax.broadcasted_iota(jnp.int32, (4 * tasks, LANES), 0)
+    lane = lax.broadcasted_iota(jnp.int32, (4 * tasks, LANES), 1)
+    values = jnp.where(lane == row // tasks, values, 0.0)
+    owner = lax.broadcasted_iota(jnp.int32, (devices, 4 * tasks), 0)
+    place = lax.broadcasted_iota(jnp.int32, (devices, 4 * tasks), 1)
+    part, task = place // tasks, place % tasks
+    index = jnp.where(part < 2, owner // (tasks // 2), owner % (tasks // 2))
+    chosen = jnp.where(task == 2 * index + part % 2, 1.0, 0.0)
+    asked = lax.dot_general(
+        chosen, values, NN, precision=lax.Precision.HIGHEST, preferred_element_type=jnp.float32
+    )
+    out_ref[...] = asked.astype(jnp.int32)
+
+
+def ask_blocks(work_blocks, block_place, devices):
+    return pl.pallas_call(
+        ask_kernel,
+        out_shape=jax.ShapeDtypeStruct((devices, LANES), jnp.int32),
+        compiler_params=pltpu.CompilerParams(vmem_limit_bytes=VMEM_BYTES),
+        name="ask_blocks",
+    )(work_blocks, block_place.reshape(-1, LANES))
 
 
 def flatten_kernel(density_ref, flat_ref):
@@ -63,26 +103,40 @@
     )(density)
 
 
-def pick_kernel(wanted_ref, flat_ref, out_ref):
+def pick_kernel(wanted_ref, flat_ref, out_ref, lines_ref, turned_ref, scalars_ref, arrived):
+    devices = lines_ref.shape[1]
+    turned = wanted_ref[...].T
+    turned_ref[...] = jnp.concatenate(
+        [turned[part // 2:part // 2 + 1] + turned[2 + part % 2:3 + part % 2] for part in range(4)] * 2, axis=0
+    )
+    copy = pltpu.make_async_copy(turned_ref, scalars_ref, arrived)
+    copy.start()
+    lines_ref[...] = turned_ref[...]
+    copy.wait()
+
     def pick(device, carry):
         for part in range(4):
-            source = pl.multiple_of(wanted_ref[device, 0, part // 2] + wanted_ref[device, 0, 2 + part % 2], 2)
+            source = pl.multiple_of(scalars_ref[part, device], 2)
             target = pl.multiple_of(SUBLANES * device + 2 * part, 2)
             out_ref[pl.ds(target, 2), :] = flat_ref[pl.ds(source, 2), :]
         return carry
 
-    lax.fori_loop(0, out_ref.shape[0] // SUBLANES, pick, 0, unroll=8)
-
-
-def pick_blocks(wanted, flat, devices):
+    lax.fori_loop(0, devices, pick, 0, unroll=8)
+
+
+def pick_blocks(wanted, flat):
+    devices = wanted.shape[0]
     return pl.pallas_call(
         pick_kernel,
-        out_shape=jax.ShapeDtypeStruct((devices * SUBLANES, LANES), jnp.float32),
-        in_specs=[
-            pl.BlockSpec(memory_space=pltpu.SMEM),
-            pl.BlockSpec(memory_space=pltpu.VMEM),
+        out_shape=(
+            jax.ShapeDtypeStruct((devices * SUBLANES, LANES), jnp.float32),
+            jax.ShapeDtypeStruct((SUBLANES, devices), jnp.int32),
+        ),
+        scratch_shapes=[
+            pltpu.VMEM((SUBLANES, devices), jnp.int32),
+            pltpu.SMEM((SUBLANES, devices), jnp.int32),
+            pltpu.SemaphoreType.DMA,
         ],
-        out_specs=pl.BlockSpec(memory_space=pltpu.VMEM),
         compiler_params=pltpu.CompilerParams(vmem_limit_bytes=VMEM_BYTES),
         name="pick_blocks",
     )(wanted, flat)
@@ -98,8 +152,7 @@
         places = []
         sums = []
         for part in range(4):
-            place = wanted_ref[device, 0, part // 2] + wanted_ref[device, 0, 2 + part % 2]
-            place = pl.ds(pl.multiple_of(place, 2), 2)
+            place = pl.ds(pl.multiple_of(wanted_ref[part, device], 2), 2)
             source = pl.multiple_of(SUBLANES * device + 2 * part, 2)
             places.append(place)
             sums.append(flat_ref[place, :] + parts_ref[pl.ds(source, 2), :])
@@ -195,7 +248,7 @@
     )(class_tables)
 
 
-def sort_kernel(count_ref, bra_ref, ket_ref, class_ref, factor_ref, columns_ref, rows_ref):
+def sort_kernel(count_ref, bra_ref, ket_ref, class_ref, factor_ref, rows_ref):
     slots = bra_ref.shape[1]
     bra, ket = bra_ref[...], ket_ref[...]
     shell_a, shell_b = bra // 32, bra % 32
@@ -233,9 +286,6 @@
     rows_ref[...] = lax.dot_general(
         fields, order, NT, precision=lax.Precision.HIGHEST, preferred_element_type=jnp.float32
     )
-    columns_ref[...] = lax.dot_general(
-        order, fields, NT, precision=lax.Precision.HIGHEST, preferred_element_type=jnp.float32
-    )
 
 
 def sort_quartets(count, bra, ket, klass, factor):
@@ -243,12 +293,9 @@
     vmem = pl.BlockSpec(memory_space=pltpu.VMEM)
     return pl.pallas_call(
         sort_kernel,
-        out_shape=(
-            jax.ShapeDtypeStruct((slots, SUBLANES), jnp.float32),
-            jax.ShapeDtypeStruct((SUBLANES, slots), jnp.float32),
-        ),
+        out_shape=jax.ShapeDtypeStruct((SUBLANES, slots), jnp.float32),
         in_specs=[pl.BlockSpec(memory_space=pltpu.SMEM)] + [vmem] * 4,
-        out_specs=(vmem, vmem),
+        out_specs=vmem,
         compiler_params=pltpu.CompilerParams(vmem_limit_bytes=VMEM_BYTES),
         name="sort_quartets",
     )(count, bra, ket, klass, factor)
@@ -258,7 +305,7 @@
 
 
 def quartet_kernel(
-    ends_ref, blocks_ref, left_ref, right_ref, columns_ref, rows_ref, tables_ref,
+    ends_ref, blocks_ref, left_ref, right_ref, rows_ref, tables_ref,
     out_ref, scaled_ref, pieces_ref, totals_ref, found_ref, values_ref,
 ):
     classes = tables_ref.shape[0]
@@ -275,7 +322,7 @@
     def step(index, carry):
         base = pl.multiple_of(index * STEP, STEP)
         here = pl.ds(base, STEP)
-        columns = columns_ref[here, :]
+        columns = rows_ref[:, here].T
         lane = lax.broadcasted_iota(jnp.int32, (STEP, pairs), 1)
         chosen = jnp.concatenate(
             [
@@ -325,14 +372,14 @@
                     * right_ref[...][None]).reshape(out_ref.shape)
 
 
-def add_quartets(ends, blocks, left, right, columns, rows, tables):
+def add_quartets(ends, blocks, left, right, rows, tables):
     lines = blocks.shape[0]
     width = tables.shape[-1]
     vmem = pl.BlockSpec(memory_space=pltpu.VMEM)
     return pl.pallas_call(
         quartet_kernel,
         out_shape=jax.ShapeDtypeStruct(blocks.shape, jnp.float32),
-        in_specs=[pl.BlockSpec(memory_space=pltpu.SMEM)] + [vmem] * 6,
+        in_specs=[pl.BlockSpec(memory_space=pltpu.SMEM)] + [vmem] * 5,
         out_specs=vmem,
         scratch_shapes=[
             pltpu.VMEM((lines, LANES), jnp.float32),
@@ -343,7 +390,7 @@
         ],
         compiler_params=pltpu.CompilerParams(vmem_limit_bytes=VMEM_BYTES),
         name="add_quartets",
-    )(ends, blocks, left, right, columns, rows, tables)
+    )(ends, blocks, left, right, rows, tables)
 
 
 def exchange(values):
@@ -366,22 +413,11 @@
     row_count = lax.axis_size("row")
     col_count = lax.axis_size("col")
     devices = row_count * col_count
-    row_blocks = density.shape[0] // SHELL
-    col_blocks = density.shape[1] // SHELL
     classes = class_tables.shape[0]
     own_tasks = work_blocks[0]
-    places = block_place[own_tasks]
-    row_part = (places % row_blocks * (2 * col_blocks)).reshape(row_count, 2)
-    col_part = (places % col_blocks * 2).reshape(col_count, 2)
-    outgoing = jnp.concatenate(
-        (
-            jnp.broadcast_to(row_part[:, None, :], (row_count, col_count, 2)),
-            jnp.broadcast_to(col_part[None, :, :], (row_count, col_count, 2)),
-        ),
-        axis=2,
-    )
-    wanted = exchange(outgoing.reshape(devices, 1, 4))
-    picked = pick_blocks(wanted, flatten_blocks(density), devices)
+    asked = ask_blocks(work_blocks, block_place, devices)
+    wanted = exchange(asked.reshape(devices, 1, LANES)).reshape(devices, LANES)
+    picked, lines = pick_blocks(wanted, flatten_blocks(density))
     blocks = exchange(picked.reshape(devices, SUBLANES, LANES))
     blocks = blocks.reshape(devices * SUBLANES, LANES)
 
@@ -393,13 +429,13 @@
     right = jnp.broadcast_to(
         scales.reshape(col_count, 1, 2, 1, 1, SHELL), (col_count, 2, 2, 2, SUBLANES, SHELL)
     ).reshape(col_count, SUBLANES, LANES)
-    columns, rows = sort_quartets(quartet_count, quartet_bra, quartet_ket, quartet_class, quartet_factor)
+    rows = sort_quartets(quartet_count, quartet_bra, quartet_ket, quartet_class, quartet_factor)
     slots = quartet_class.shape[1]
     within = jnp.where(jnp.arange(slots) < quartet_count[0], quartet_class[0], classes)
     ends = jnp.sum((within[None, :] <= jnp.arange(classes)[:, None]).astype(jnp.int32), axis=1)
-    summed = add_quartets(ends, blocks, left, right, columns, rows, tables)
+    summed = add_quartets(ends, blocks, left, right, rows, tables)
     returned = exchange(summed.reshape(devices, SUBLANES, LANES))
-    return merge_blocks(wanted, returned.reshape(devices * SUBLANES, LANES), core_hamiltonian)
+    return merge_blocks(lines, returned.reshape(devices * SUBLANES, LANES), core_hamiltonian)
 
 
 def solution(mesh):

time: 135 us -> 130 us (0.963)
  Pallas kernels: 28.6 us -> 24.9 us
  local copies, waits for them, and re-layouts: 7.43 us -> 5.36 us
  waiting for transfers between devices: 29.3 us -> 30.8 us
    pallas_call x1, Pallas kernels: 7.28 us -> 5.34 us  [merge_blocks(): pl.pallas_call(merge_kernel, out_shape=jax.ShapeDtypeStruct(core.shape, j...]
    pallas_call x2 -> x3, Pallas kernels: 7.22 us -> 5.48 us  [the longest x1 3.15 us: pick_blocks(): pl.pallas_call(pick_kernel, out_shape=(jax.ShapeDtypeStruct((devices * SU...]
    all_to_all x2, waiting for transfers between devices: 29.3 us -> 30.8 us  [exchange(): return lax.all_to_all(values, AXES, split_axis=0, concat_axis=0, tiled=True)]
where the time goes in v4:
time: 130 us; the launch traced here: 129 us
  blocking collectives  44.5 us (34%)
  waiting for transfers between devices  30.8 us (24%)
  Pallas kernels  24.9 us (19%)
  starting transfers between devices  22.7 us (17%)
  local copies, waits for them, and re-layouts  5.36 us (4%)
    all_to_all x1, blocking collectives, exchange(): return lax.all_to_all(values, AXES, split_axis=0, concat_axis=0, tiled=True)  44.5 us
    all_to_all x2, waiting for transfers between devices, exchange(): return lax.all_to_all(values, AXES, split_axis=0, concat_axis=0, tiled=True)  30.8 us
    all_to_all x2, starting transfers between devices, exchange(): return lax.all_to_all(values, AXES, split_axis=0, concat_axis=0, tiled=True)  22.7 us
    pallas_call x1, Pallas kernels, make_tables(): pl.pallas_call(table_kernel, grid=(classes,), out_shape=jax.ShapeDtypeStr...  6.38 us
    pallas_call x1, Pallas kernels, add_quartets(): pl.pallas_call(quartet_kernel, out_shape=jax.ShapeDtypeStruct(blocks.shap...  6.17 us
    pallas_call x1, Pallas kernels, merge_blocks(): pl.pallas_call(merge_kernel, out_shape=jax.ShapeDtypeStruct(core.shape, j...  5.34 us
    unnamed x22, local copies, waits for them, and re-layouts  4.02 us
    pallas_call x1, Pallas kernels, pick_blocks(): pl.pallas_call(pick_kernel, out_shape=(jax.ShapeDtypeStruct((devices * SU...  3.15 us
  transfers between devices with their start and end apart: 2, of which 2 were waited for; matrix products, arithmetic and copies ran while one was open for 1% of the time, Pallas kernels for 7%

profile of v4, /device:TPU:1, one launch (start us, length us, event | category | flops | bytes accessed | tf_op | source)
XLA Modules:
  0.0 129.3 jit_solution(18111872419535827184)
XLA Ops:
  0.0 0.7 copy-done.4
  0.7 0.7 copy-done.8
  1.3 1.2 ask_blocks.1
  2.5 15.7 %all-to-all-start = ((s32[256,1,128]{2,1,0:T(1,128)}), s32[256,1,128]{2,1,0:T(1,128)S(1)}, u32[]{:S(2)}, u32[]{:S(2)}) async-start(s32[256,1,128]{2,1,0:T(1,128)} %bitcast.2), calls=%async_computation | async-start | bytes 262144 | tf_op jit(solution)/shard_map/all_to_all | solution.py:397
  18.2 0.0 copy-start
  18.2 1.4 %copy-done = f32[640,640]{1,0:T(8,128)S(1)} copy-done((f32[640,640]{1,0:T(8,128)S(1)}, f32[640,640]{1,0:T(8,128)}, u32[]{:S(2)}) %copy-start) | copy-done | bytes 1638424
  19.6 1.5 %flatten_blocks.1.flat_ref = f32[3200,128]{1,0:T(8,128)S(1)} custom-call(f32[640,640]{1,0:T(8,128)S(1)} %copy-done), custom_call_target="tpu_custom_call" | custom-call | tf_op jit(solution)/shard_map/flatten_blocks/pallas_call | solution.py:98
  21.2 10.1 %all-to-all-done = s32[256,1,128]{2,1,0:T(1,128)S(1)} async-done(((s32[256,1,128]{2,1,0:T(1,128)}), s32[256,1,128]{2,1,0:T(1,128)S(1)}, u32[]{:S(2)}, u32[]{:S(2)}) %all-to-all-start) | async-done | bytes 131104 | tf_op jit(solution)/shard_map/all_to_all | solution.py:397
  31.3 3.1 %pick_blocks.1 = (f32[2048,128]{1,0:T(8,128)}, s32[8,256]{1,0:T(8,128)S(1)}) custom-call(s32[256,128]{1,0:T(8,128)S(1)} %bitcast.23, f32[3200,128]{1,0:T(8,128)S(1)} %flatten_blocks.1.flat_ref), custom_call_target="tpu_custom_call" | custom-call | tf_op jit(solution)/shard_map/pick_blocks/pallas_call | solution.py:129
  34.4 0.0 copy-start.9
  34.4 7.1 %all-to-all-start.1 = ((f32[256,8,128]{2,1,0:T(8,128)}), f32[256,8,128]{2,1,0:T(8,128)}, u32[]{:S(2)}, u32[]{:S(2)}) async-start(f32[256,8,128]{2,1,0:T(8,128)} %bitcast.6), calls=%async_computation.1 | async-start | bytes 2097152 | tf_op jit(solution)/shard_map/all_to_all | solution.py:397
  42.2 0.0 copy-done.10
  42.2 0.1 reshape.74
  42.3 0.0 copy-done.9
  42.4 0.6 gather_fusion
  42.9 0.1 broadcast_in_dim.22
  43.0 0.1 broadcast_in_dim.23
  43.2 0.2 reshape.75.left_ref
  43.4 0.2 reshape.76.right_ref
  43.6 0.0 copy-start.2
  43.6 1.2 copy-done.2
  44.8 6.4 %make_tables.1.tables_ref = bf16[4,3,2,256,256]{4,3,2,1,0:T(8,128)(2,1)S(1)} custom-call(f32[4,256,256]{2,1,0:T(8,128)S(1)} %copy-done.2), custom_call_target="tpu_custom_call" | custom-call | tf_op jit(solution)/shard_map/make_tables/pallas_call | solution.py:235
  51.2 0.0 copy-done.3
  51.2 0.0 copy-done.5
  51.3 1.2 sort_quartets.1.rows_ref
  52.4 0.1 convert_reduce_fusion.ends_ref
  52.6 20.7 %all-to-all-done.1 = f32[256,8,128]{2,1,0:T(8,128)} async-done(((f32[256,8,128]{2,1,0:T(8,128)}), f32[256,8,128]{2,1,0:T(8,128)}, u32[]{:S(2)}, u32[]{:S(2)}) %all-to-all-start.1) | async-done | bytes 1048608 | tf_op jit(solution)/shard_map/all_to_all | solution.py:397
  73.3 6.2 %add_quartets.1 = f32[2048,128]{1,0:T(8,128)S(1)} custom-call(s32[4]{0:T(128)S(1)} %convert_reduce_fusion.ends_ref, f32[2048,128]{1,0:T(8,128)} %bitcast.7.blocks_ref, f32[16,8,128]{2,1,0:T(8,128)S(1)} %reshape.75.left_ref, f32[16,8,128]{2,1,0:T(8,128)S(1)} %reshape.76.right_ref, f32[8,512]{1,0:T(8,128)S(1)} %sort_quartets.1.rows_ref, ...), custom_call_target="tpu_custom_call" | custom-call | tf_op jit(solution)/shard_map/add_quartets/pallas_call | solution.py:379
  79.5 0.0 copy-start.1
  79.5 44.5 %all_to_all.15 = f32[256,8,128]{2,1,0:T(8,128)S(1)} all-to-all(f32[256,8,128]{2,1,0:T(8,128)S(1)} %bitcast.21), channel_id=1, replica_groups=mesh['row'=16,'col'=16] {'row','col'}, dimensions={0} | all-to-all | bytes 2097152 | tf_op jit(solution)/shard_map/all_to_all | solution.py:397
  124.0 0.0 copy-done.1
  124.0 5.3 %merge_blocks.1 = f32[640,640]{1,0:T(8,128)} custom-call(s32[8,256]{1,0:T(8,128)S(1)} %get-tuple-element.7.wanted_ref, f32[2048,128]{1,0:T(8,128)S(1)} %bitcast.22, f32[640,640]{1,0:T(8,128)S(1)} %copy-done.1), custom_call_target="tpu_custom_call" | custom-call | tf_op jit(solution)/shard_map/merge_blocks/pallas_call | solution.py:180
  (13 shorter events, 0.1 us)
Async XLA Ops:
  0.0 0.7 copy-start.4
  0.7 0.7 copy-start.8
  2.5 28.7 %all-to-all-start = ((s32[256,1,128]{2,1,0:T(1,128)}), s32[256,1,128]{2,1,0:T(1,128)S(1)}, u32[]{:S(2)}, u32[]{:S(2)}) async-start(s32[256,1,128]{2,1,0:T(1,128)} %bitcast.2), calls=%async_computation | async-start | bytes 262144 | tf_op jit(solution)/shard_map/all_to_all | solution.py:397
  18.2 1.4 %copy-start = (f32[640,640]{1,0:T(8,128)S(1)}, f32[640,640]{1,0:T(8,128)}, u32[]{:S(2)}) copy-start(f32[640,640]{1,0:T(8,128)} %density_ref.1) | copy-start | bytes 4915204
  31.3 10.9 %copy-start.10 = (f32[10240]{0:T(1024)S(1)}, f32[10240]{0:T(1024)}, u32[]{:S(2)}) copy-start(f32[10240]{0:T(1024)} %param.14) | copy-start | bytes 122884
  34.4 7.9 %copy-start.9 = (s32[1,32]{1,0:T(1,128)S(1)}, s32[1,32]{1,0:T(1,128)}, u32[]{:S(2)}) copy-start(s32[1,32]{1,0:T(1,128)} %work_ref.1) | copy-start | bytes 388
  34.4 38.9 %all-to-all-start.1 = ((f32[256,8,128]{2,1,0:T(8,128)}), f32[256,8,128]{2,1,0:T(8,128)}, u32[]{:S(2)}, u32[]{:S(2)}) async-start(f32[256,8,128]{2,1,0:T(8,128)} %bitcast.6), calls=%async_computation.1 | async-start | bytes 2097152 | tf_op jit(solution)/shard_map/all_to_all | solution.py:397
  43.6 1.2 copy-start.2
  44.8 6.4 %copy-start.3 = (s32[1,512]{1,0:T(1,128)S(1)}, s32[1,512]{1,0:T(1,128)}, u32[]{:S(2)}) copy-start(s32[1,512]{1,0:T(1,128)} %class_ref.1) | copy-start | bytes 6148
  44.8 6.4 %copy-start.5 = (s32[1,512]{1,0:T(1,128)S(1)}, s32[1,512]{1,0:T(1,128)}, u32[]{:S(2)}) copy-start(s32[1,512]{1,0:T(1,128)} %bra_ref.1) | copy-start | bytes 6148
  44.8 6.4 %copy-start.6 = (s32[1,512]{1,0:T(1,128)S(1)}, s32[1,512]{1,0:T(1,128)}, u32[]{:S(2)}) copy-start(s32[1,512]{1,0:T(1,128)} %ket_ref.1) | copy-start | bytes 6148
  44.8 6.4 %copy-start.7 = (f32[1,512]{1,0:T(1,128)S(1)}, f32[1,512]{1,0:T(1,128)}, u32[]{:S(2)}) copy-start(f32[1,512]{1,0:T(1,128)} %factor_ref.1) | copy-start | bytes 6148
  79.5 44.5 %copy-start.1 = (f32[640,640]{1,0:T(8,128)S(1)}, f32[640,640]{1,0:T(8,128)}, u32[]{:S(2)}) copy-start(f32[640,640]{1,0:T(8,128)} %core_ref.1) | copy-start | bytes 4915204

commit v5 on v4

--- a/solution.py
+++ b/solution.py
@@ -11,7 +11,7 @@
 LANES = 128
 SUBLANES = 8
 STRIPE = 40
-VMEM_BYTES = 16 << 20
+VMEM_BYTES = 24 << 20
 GROUPS = LANES // SHELL
 AXES = ("row", "col")
 NT = (((1,), (1,)), ((), ()))
@@ -71,7 +71,7 @@
     return pl.pallas_call(
         ask_kernel,
         out_shape=jax.ShapeDtypeStruct((devices, LANES), jnp.int32),
-        compiler_params=pltpu.CompilerParams(vmem_limit_bytes=VMEM_BYTES),
+        compiler_params=pltpu.CompilerParams(vmem_limit_bytes=60 << 20),
         name="ask_blocks",
     )(work_blocks, block_place.reshape(-1, LANES))
 
@@ -301,16 +301,22 @@
     )(count, bra, ket, klass, factor)
 
 
-STEP = 128
+STEP = 256
+TILE = 160
+
+
+def one_hot(index, number):
+    return jnp.where(number == index.astype(jnp.int32), 1.0, 0.0).astype(jnp.bfloat16)
 
 
 def quartet_kernel(
     ends_ref, blocks_ref, left_ref, right_ref, rows_ref, tables_ref,
-    out_ref, scaled_ref, pieces_ref, totals_ref, found_ref, values_ref,
+    out_ref, scaled_ref, pieces_ref, totals_ref, found_ref, values_ref, factors_ref,
 ):
     classes = tables_ref.shape[0]
     pairs = pieces_ref.shape[0]
     width = totals_ref.shape[1]
+    kinds = range(6)
     scaled_ref[...] = (blocks_ref[...].reshape(16, 16, SUBLANES, LANES) * left_ref[...][:, None]
                        * right_ref[...][None]).reshape(scaled_ref.shape)
     for half in range(2):
@@ -318,54 +324,58 @@
         pieces_ref[:, LANES * half:LANES * (half + 1)] = high
         pieces_ref[:, width + LANES * half:width + LANES * (half + 1)] = low
     totals_ref[...] = jnp.zeros_like(totals_ref)
-
-    def step(index, carry):
-        base = pl.multiple_of(index * STEP, STEP)
-        here = pl.ds(base, STEP)
+    steps = (ends_ref[classes - 1] + STEP - 1) // STEP
+
+    def find(index, carry):
+        here = pl.ds(pl.multiple_of(index * STEP, STEP), STEP)
         columns = rows_ref[:, here].T
-        lane = lax.broadcasted_iota(jnp.int32, (STEP, pairs), 1)
-        chosen = jnp.concatenate(
-            [
-                jnp.where(lane == columns[:, kind:kind + 1].astype(jnp.int32), 1.0, 0.0).astype(jnp.bfloat16)
-                for kind in range(6)
-            ],
-            axis=0,
-        )
+        number = lax.broadcasted_iota(jnp.int32, (STEP, pairs), 1)
+        chosen = jnp.concatenate([one_hot(columns[:, kind:kind + 1], number) for kind in kinds], axis=0)
         found = dot(chosen, pieces_ref[...], NN).astype(jnp.bfloat16)
-        for kind in range(6):
+        for kind in kinds:
             part = slice(STEP * kind, STEP * (kind + 1))
-            found_ref[kind, :STEP] = found[part, :width]
-            found_ref[kind, STEP:] = found[part, width:]
-        values_ref[...] = jnp.zeros_like(values_ref)
-        for klass in range(classes):
-            begin = 0 if klass == 0 else ends_ref[klass - 1]
-
-            @pl.when((begin < base + STEP) & (ends_ref[klass] > base) & (begin < ends_ref[klass]))
-            def _():
-                factor = jnp.where(columns[:, 6:7] == klass, columns[:, 7:8], 0.0)
-                for kind in range(6):
-                    part = slice(STEP * kind, STEP * (kind + 1))
-                    dims = NT if kind % 2 == 0 else NN
-                    product = dot(found_ref[kind], tables_ref[klass, kind // 2, 0], dims)
-                    product = product[:STEP] + product[STEP:]
-                    product += dot(found_ref[kind, :STEP], tables_ref[klass, kind // 2, 1], dims)
-                    values_ref[part, :] += product * (factor if kind < 2 else -0.5 * factor)
-
-        high, low = split(values_ref[...])
-        sublane = lax.broadcasted_iota(jnp.int32, (pairs, STEP), 0)
-        chosen = jnp.concatenate(
-            [
-                jnp.where(sublane == rows_ref[kind ^ 1:(kind ^ 1) + 1, here].astype(jnp.int32), 1.0, 0.0).astype(
-                    jnp.bfloat16
-                )
-                for kind in range(6)
-            ],
-            axis=1,
-        )
+            found_ref[kind, 0, here, :] = found[part, :width]
+            found_ref[kind, 1, here, :] = found[part, width:]
+            values_ref[kind, here, :] = jnp.zeros((STEP, width), jnp.float32)
+        factors_ref[here, :] = jnp.broadcast_to(columns[:, 7:8], (STEP, LANES))
+        return carry
+
+    lax.fori_loop(0, steps, find, 0)
+
+    for klass in range(classes):
+        begin = 0 if klass == 0 else ends_ref[klass - 1]
+        end = ends_ref[klass]
+        base = begin // 16 * 16
+
+        def multiply(index, carry):
+            start = pl.multiple_of(base + index * TILE, 16)
+            here = pl.ds(start, TILE)
+            slot = start + lax.broadcasted_iota(jnp.int32, (TILE, width), 0)
+            mine = (slot >= begin) & (slot < end)
+            factor = factors_ref[here, :]
+            factor = jnp.concatenate((factor, factor), axis=1)
+            for kind in kinds:
+                form = kind // 2
+                dims = NT if kind % 2 == 0 else NN
+                high, low = found_ref[kind, 0, here, :], found_ref[kind, 1, here, :]
+                product = dot(jnp.concatenate((high, low), axis=0), tables_ref[klass, form, 0], dims)
+                product = product[:TILE] + product[TILE:]
+                product += dot(high, tables_ref[klass, form, 1], dims)
+                product *= factor if kind < 2 else -0.5 * factor
+                values_ref[kind, here, :] = jnp.where(mine, product, values_ref[kind, here, :])
+            return carry
+
+        lax.fori_loop(0, jnp.where(begin < end, (end - base + TILE - 1) // TILE, 0), multiply, 0)
+
+    def add(index, carry):
+        here = pl.ds(pl.multiple_of(index * STEP, STEP), STEP)
+        number = lax.broadcasted_iota(jnp.int32, (pairs, STEP), 0)
+        chosen = jnp.concatenate([one_hot(rows_ref[kind ^ 1:(kind ^ 1) + 1, here], number) for kind in kinds], axis=1)
+        high, low = split(jnp.concatenate([values_ref[kind, here, :] for kind in kinds], axis=0))
         totals_ref[...] += dot(chosen, high, NN) + dot(chosen, low, NN)
         return carry
 
-    lax.fori_loop(0, (ends_ref[classes - 1] + STEP - 1) // STEP, step, 0)
+    lax.fori_loop(0, steps, add, 0)
     for half in range(2):
         scaled_ref[pl.ds(half, pairs, stride=2), :] = totals_ref[:, LANES * half:LANES * (half + 1)]
     out_ref[...] = (scaled_ref[...].reshape(16, 16, SUBLANES, LANES) * left_ref[...][:, None]
@@ -374,6 +384,7 @@
 
 def add_quartets(ends, blocks, left, right, rows, tables):
     lines = blocks.shape[0]
+    padded = rows.shape[1] + TILE
     width = tables.shape[-1]
     vmem = pl.BlockSpec(memory_space=pltpu.VMEM)
     return pl.pallas_call(
@@ -385,8 +396,9 @@
             pltpu.VMEM((lines, LANES), jnp.float32),
             pltpu.VMEM((lines // 2, 2 * width), jnp.bfloat16),
             pltpu.VMEM((lines // 2, width), jnp.float32),
-            pltpu.VMEM((6, 2 * STEP, width), jnp.bfloat16),
-            pltpu.VMEM((6 * STEP, width), jnp.float32),
+            pltpu.VMEM((6, 2, padded, width), jnp.bfloat16),
+            pltpu.VMEM((6, padded, width), jnp.float32),
+            pltpu.VMEM((padded, LANES), jnp.float32),
         ],
         compiler_params=pltpu.CompilerParams(vmem_limit_bytes=VMEM_BYTES),
         name="add_quartets",

time: 130 us -> 127 us (0.977)
  blocking collectives: 44.5 us -> 40.3 us
  Pallas kernels: 24.9 us -> 27.7 us
  local copies, waits for them, and re-layouts: 5.36 us -> 4.02 us
    all_to_all x1, blocking collectives: 44.5 us -> 40.3 us  [exchange(): return lax.all_to_all(values, AXES, split_axis=0, concat_axis=0, tiled=True)]
    pallas_call x1, Pallas kernels: 6.17 us -> 8.24 us  [add_quartets(): pl.pallas_call(quartet_kernel, out_shape=jax.ShapeDtypeStruct(blocks.shap...]
    unnamed x22 -> x18, local copies, waits for them, and re-layouts: 4.02 us -> 2.68 us
where the time goes in v5:
time: 127 us
  blocking collectives  40.3 us (32%)
  waiting for transfers between devices  30.8 us (24%)
  Pallas kernels  27.7 us (22%)
  starting transfers between devices  22.7 us (18%)
  local copies, waits for them, and re-layouts  4.02 us (3%)
    all_to_all x1, blocking collectives, exchange(): return lax.all_to_all(values, AXES, split_axis=0, concat_axis=0, tiled=True)  40.3 us
    all_to_all x2, waiting for transfers between devices, exchange(): return lax.all_to_all(values, AXES, split_axis=0, concat_axis=0, tiled=True)  30.8 us
    all_to_all x2, starting transfers between devices, exchange(): return lax.all_to_all(values, AXES, split_axis=0, concat_axis=0, tiled=True)  22.7 us
    pallas_call x1, Pallas kernels, add_quartets(): pl.pallas_call(quartet_kernel, out_shape=jax.ShapeDtypeStruct(blocks.shap...  8.24 us
    pallas_call x1, Pallas kernels, make_tables(): pl.pallas_call(table_kernel, grid=(classes,), out_shape=jax.ShapeDtypeStr...  6.38 us
    pallas_call x1, Pallas kernels, merge_blocks(): pl.pallas_call(merge_kernel, out_shape=jax.ShapeDtypeStruct(core.shape, j...  5.34 us
    pallas_call x1, Pallas kernels, pick_blocks(): pl.pallas_call(pick_kernel, out_shape=(jax.ShapeDtypeStruct((devices * SU...  3.15 us
    unnamed x18, local copies, waits for them, and re-layouts  2.68 us
  transfers between devices with their start and end apart: 2, of which 2 were waited for; matrix products, arithmetic and copies ran while one was open for 1% of the time, Pallas kernels for 7%

profile of v5, /device:TPU:1, one launch (start us, length us, event | category | flops | bytes accessed | tf_op | source)
XLA Modules:
  0.0 126.6 jit_solution(16109296399229122892)
XLA Ops:
  0.0 1.9 %ask_blocks.1 = s32[256,128]{1,0:T(8,128)} custom-call(s32[1,32]{1,0:T(1,128)} %work_ref.1, s32[5,128]{1,0:T(8,128)} %bitcast.27), custom_call_target="tpu_custom_call" | custom-call | tf_op jit(solution)/shard_map/ask_blocks/pallas_call | solution.py:71
  1.9 15.7 %all-to-all-start = ((s32[256,1,128]{2,1,0:T(1,128)}), s32[256,1,128]{2,1,0:T(1,128)S(1)}, u32[]{:S(2)}, u32[]{:S(2)}) async-start(s32[256,1,128]{2,1,0:T(1,128)} %bitcast.24), calls=%async_computation | async-start | bytes 262144 | tf_op jit(solution)/shard_map/all_to_all | solution.py:409
  17.6 0.0 copy-start
  17.6 1.4 %copy-done = f32[640,640]{1,0:T(8,128)S(1)} copy-done((f32[640,640]{1,0:T(8,128)S(1)}, f32[640,640]{1,0:T(8,128)}, u32[]{:S(2)}) %copy-start) | copy-done | bytes 1638424
  19.0 1.5 %flatten_blocks.1.flat_ref = f32[3200,128]{1,0:T(8,128)S(1)} custom-call(f32[640,640]{1,0:T(8,128)S(1)} %copy-done), custom_call_target="tpu_custom_call" | custom-call | tf_op jit(solution)/shard_map/flatten_blocks/pallas_call | solution.py:98
  20.5 10.1 %all-to-all-done = s32[256,1,128]{2,1,0:T(1,128)S(1)} async-done(((s32[256,1,128]{2,1,0:T(1,128)}), s32[256,1,128]{2,1,0:T(1,128)S(1)}, u32[]{:S(2)}, u32[]{:S(2)}) %all-to-all-start) | async-done | bytes 131104 | tf_op jit(solution)/shard_map/all_to_all | solution.py:409
  30.7 3.1 %pick_blocks.1 = (f32[2048,128]{1,0:T(8,128)}, s32[8,256]{1,0:T(8,128)S(1)}) custom-call(s32[256,128]{1,0:T(8,128)S(1)} %bitcast.23, f32[3200,128]{1,0:T(8,128)S(1)} %flatten_blocks.1.flat_ref), custom_call_target="tpu_custom_call" | custom-call | tf_op jit(solution)/shard_map/pick_blocks/pallas_call | solution.py:129
  33.8 0.0 copy-start.8
  33.8 7.1 %all-to-all-start.1 = ((f32[256,8,128]{2,1,0:T(8,128)}), f32[256,8,128]{2,1,0:T(8,128)}, u32[]{:S(2)}, u32[]{:S(2)}) async-start(f32[256,8,128]{2,1,0:T(8,128)} %bitcast.6), calls=%async_computation.1 | async-start | bytes 2097152 | tf_op jit(solution)/shard_map/all_to_all | solution.py:409
  41.5 0.0 copy-done.7
  41.5 0.1 reshape.74
  41.7 0.0 copy-done.8
  41.7 0.6 gather_fusion
  42.3 0.1 broadcast_in_dim.22
  42.4 0.1 broadcast_in_dim.23
  42.5 0.2 reshape.75.left_ref
  42.8 0.2 reshape.76.right_ref
  43.0 0.0 copy-start.2
  43.0 1.2 copy-done.2
  44.2 6.4 %make_tables.1.tables_ref = bf16[4,3,2,256,256]{4,3,2,1,0:T(8,128)(2,1)S(1)} custom-call(f32[4,256,256]{2,1,0:T(8,128)S(1)} %copy-done.2), custom_call_target="tpu_custom_call" | custom-call | tf_op jit(solution)/shard_map/make_tables/pallas_call | solution.py:235
  50.6 0.0 copy-done.3
  50.6 0.0 copy-done.4
  50.6 0.0 copy-done.5
  50.6 0.0 copy-done.6
  50.6 1.2 sort_quartets.1.rows_ref
  51.8 0.1 convert_reduce_fusion.ends_ref
  51.9 20.7 %all-to-all-done.1 = f32[256,8,128]{2,1,0:T(8,128)} async-done(((f32[256,8,128]{2,1,0:T(8,128)}), f32[256,8,128]{2,1,0:T(8,128)}, u32[]{:S(2)}, u32[]{:S(2)}) %all-to-all-start.1) | async-done | bytes 1048608 | tf_op jit(solution)/shard_map/all_to_all | solution.py:409
  72.7 8.2 %add_quartets.1 = f32[2048,128]{1,0:T(8,128)S(1)} custom-call(s32[4]{0:T(128)S(1)} %convert_reduce_fusion.ends_ref, f32[2048,128]{1,0:T(8,128)} %bitcast.7.blocks_ref, f32[16,8,128]{2,1,0:T(8,128)S(1)} %reshape.75.left_ref, f32[16,8,128]{2,1,0:T(8,128)S(1)} %reshape.76.right_ref, f32[8,512]{1,0:T(8,128)S(1)} %sort_quartets.1.rows_ref, ...), custom_call_target="tpu_custom_call" | custom-call | tf_op jit(solution)/shard_map/add_quartets/pallas_call | solution.py:390
  80.9 0.0 copy-start.1
  80.9 40.3 %all_to_all.15 = f32[256,8,128]{2,1,0:T(8,128)S(1)} all-to-all(f32[256,8,128]{2,1,0:T(8,128)S(1)} %bitcast.21), channel_id=1, replica_groups=mesh['row'=16,'col'=16] {'row','col'}, dimensions={0} | all-to-all | bytes 2097152 | tf_op jit(solution)/shard_map/all_to_all | solution.py:409
  121.2 0.0 copy-done.1
  121.2 5.3 %merge_blocks.1 = f32[640,640]{1,0:T(8,128)} custom-call(s32[8,256]{1,0:T(8,128)S(1)} %get-tuple-element.7.wanted_ref, f32[2048,128]{1,0:T(8,128)S(1)} %bitcast.22, f32[640,640]{1,0:T(8,128)S(1)} %copy-done.1), custom_call_target="tpu_custom_call" | custom-call | tf_op jit(solution)/shard_map/merge_blocks/pallas_call | solution.py:180
  (9 shorter events, 0.1 us)
Async XLA Ops:
  1.9 28.7 %all-to-all-start = ((s32[256,1,128]{2,1,0:T(1,128)}), s32[256,1,128]{2,1,0:T(1,128)S(1)}, u32[]{:S(2)}, u32[]{:S(2)}) async-start(s32[256,1,128]{2,1,0:T(1,128)} %bitcast.24), calls=%async_computation | async-start | bytes 262144 | tf_op jit(solution)/shard_map/all_to_all | solution.py:409
  17.6 1.4 %copy-start = (f32[640,640]{1,0:T(8,128)S(1)}, f32[640,640]{1,0:T(8,128)}, u32[]{:S(2)}) copy-start(f32[640,640]{1,0:T(8,128)} %density_ref.1) | copy-start | bytes 4915204
  30.6 10.9 %copy-start.7 = (f32[10240]{0:T(1024)S(1)}, f32[10240]{0:T(1024)}, u32[]{:S(2)}) copy-start(f32[10240]{0:T(1024)} %param.14) | copy-start | bytes 122884
  33.8 7.9 %copy-start.8 = (s32[1,32]{1,0:T(1,128)S(1)}, s32[1,32]{1,0:T(1,128)}, u32[]{:S(2)}) copy-start(s32[1,32]{1,0:T(1,128)} %work_ref.1) | copy-start | bytes 388
  33.8 38.9 %all-to-all-start.1 = ((f32[256,8,128]{2,1,0:T(8,128)}), f32[256,8,128]{2,1,0:T(8,128)}, u32[]{:S(2)}, u32[]{:S(2)}) async-start(f32[256,8,128]{2,1,0:T(8,128)} %bitcast.6), calls=%async_computation.1 | async-start | bytes 2097152 | tf_op jit(solution)/shard_map/all_to_all | solution.py:409
  43.0 1.2 copy-start.2
  44.2 6.4 %copy-start.3 = (s32[1,512]{1,0:T(1,128)S(1)}, s32[1,512]{1,0:T(1,128)}, u32[]{:S(2)}) copy-start(s32[1,512]{1,0:T(1,128)} %class_ref.1) | copy-start | bytes 6148
  44.2 6.4 %copy-start.4 = (s32[1,512]{1,0:T(1,128)S(1)}, s32[1,512]{1,0:T(1,128)}, u32[]{:S(2)}) copy-start(s32[1,512]{1,0:T(1,128)} %bra_ref.1) | copy-start | bytes 6148
  44.2 6.4 %copy-start.5 = (s32[1,512]{1,0:T(1,128)S(1)}, s32[1,512]{1,0:T(1,128)}, u32[]{:S(2)}) copy-start(s32[1,512]{1,0:T(1,128)} %ket_ref.1) | copy-start | bytes 6148
  44.2 6.4 %copy-start.6 = (f32[1,512]{1,0:T(1,128)S(1)}, f32[1,512]{1,0:T(1,128)}, u32[]{:S(2)}) copy-start(f32[1,512]{1,0:T(1,128)} %factor_ref.1) | copy-start | bytes 6148
  80.9 40.3 %copy-start.1 = (f32[640,640]{1,0:T(8,128)S(1)}, f32[640,640]{1,0:T(8,128)}, u32[]{:S(2)}) copy-start(f32[640,640]{1,0:T(8,128)} %core_ref.1) | copy-start | bytes 4915204

commit v6 on v5

--- a/solution.py
+++ b/solution.py
@@ -142,25 +142,26 @@
     )(wanted, flat)
 
 
-def merge_kernel(wanted_ref, parts_ref, core_ref, out_ref, flat_ref):
+def merge_kernel(wanted_ref, parts_ref, core_ref, out_ref, flat_ref, other_ref, near_ref, sent):
     row_blocks = core_ref.shape[0] // SHELL
     col_blocks = core_ref.shape[1] // SHELL
     devices = parts_ref.shape[0] // SUBLANES
     flat_ref[...] = jnp.zeros_like(flat_ref)
-
-    def add(device, carry):
-        places = []
-        sums = []
-        for part in range(4):
-            place = pl.ds(pl.multiple_of(wanted_ref[part, device], 2), 2)
-            source = pl.multiple_of(SUBLANES * device + 2 * part, 2)
-            places.append(place)
-            sums.append(flat_ref[place, :] + parts_ref[pl.ds(source, 2), :])
-        for place, value in zip(places, sums):
-            flat_ref[place, :] = value
-        return carry
-
-    lax.fori_loop(0, devices, add, 0, unroll=8)
+    other_ref[...] = jnp.zeros_like(other_ref)
+
+    def add(pair, carry):
+        todo = []
+        for which, ref in enumerate((flat_ref, other_ref)):
+            device = 2 * pair + which
+            for part in range(4):
+                place = pl.ds(pl.multiple_of(wanted_ref[part, device], 2), 2)
+                source = pl.multiple_of(SUBLANES * device + 2 * part, 2)
+                todo.append((ref, place, ref[place, :] + parts_ref[pl.ds(source, 2), :]))
+        for ref, place, value in todo:
+            ref[place, :] = value
+        return carry
+
+    lax.fori_loop(0, devices // 2, add, 0, unroll=8)
 
     def unflatten(block, carry):
         for half in range(2):
@@ -168,11 +169,19 @@
             for tile in range(col_blocks // GROUPS):
                 lanes = slice(tile * LANES, (tile + 1) * LANES)
                 place = (block * col_blocks + tile * GROUPS) * 2 + half
-                values = swap_groups(flat_ref[pl.ds(place, SUBLANES, stride=2), :])
-                out_ref[pl.ds(start, SUBLANES), lanes] = core_ref[pl.ds(start, SUBLANES), lanes] + values
-        return carry
-
-    lax.fori_loop(0, row_blocks, unflatten, 0, unroll=8)
+                spread = pl.ds(place, SUBLANES, stride=2)
+                values = swap_groups(flat_ref[spread, :] + other_ref[spread, :])
+                near_ref[pl.ds(start, SUBLANES), lanes] = core_ref[pl.ds(start, SUBLANES), lanes] + values
+        return carry
+
+    copies = []
+    for chunk in range(row_blocks // GROUPS):
+        lax.fori_loop(chunk * GROUPS, (chunk + 1) * GROUPS, unflatten, 0, unroll=GROUPS)
+        rows = pl.ds(chunk * LANES, LANES)
+        copies.append(pltpu.make_async_copy(near_ref.at[rows], out_ref.at[rows], sent.at[chunk]))
+        copies[-1].start()
+    for copy in copies:
+        copy.wait()
 
 
 def merge_blocks(wanted, parts, core):
@@ -185,8 +194,13 @@
             pl.BlockSpec(memory_space=pltpu.VMEM),
             pl.BlockSpec(memory_space=pltpu.VMEM),
         ],
-        out_specs=pl.BlockSpec(memory_space=pltpu.VMEM),
-        scratch_shapes=[pltpu.VMEM((2 * blocks, LANES), jnp.float32)],
+        out_specs=pl.BlockSpec(memory_space=pl.ANY),
+        scratch_shapes=[
+            pltpu.VMEM((2 * blocks, LANES), jnp.float32),
+            pltpu.VMEM((2 * blocks, LANES), jnp.float32),
+            pltpu.VMEM(core.shape, jnp.float32),
+            pltpu.SemaphoreType.DMA((core.shape[0] // LANES,)),
+        ],
         compiler_params=pltpu.CompilerParams(vmem_limit_bytes=VMEM_BYTES),
         name="merge_blocks",
     )(wanted, parts, core)

time: 127 us -> 126 us (level)
  blocking collectives: 40.3 us -> 36.6 us
  Pallas kernels: 27.7 us -> 30.2 us
    pallas_call x1, Pallas kernels: 8.24 us -> 12 us  [add_quartets(): pl.pallas_call(quartet_kernel, out_shape=jax.ShapeDtypeStruct(blocks.shap...]
    all_to_all x1, blocking collectives: 40.3 us -> 36.6 us  [exchange(): return lax.all_to_all(values, AXES, split_axis=0, concat_axis=0, tiled=True)]
where the time goes in v6:
time: 126 us; the launch traced here: 125 us
  blocking collectives  36.6 us (29%)
  waiting for transfers between devices  30.8 us (24%)
  Pallas kernels  30.2 us (24%)
  starting transfers between devices  22.7 us (18%)
  local copies, waits for them, and re-layouts  4.02 us (3%)
    all_to_all x1, blocking collectives, exchange(): return lax.all_to_all(values, AXES, split_axis=0, concat_axis=0, tiled=True)  36.6 us
    all_to_all x2, waiting for transfers between devices, exchange(): return lax.all_to_all(values, AXES, split_axis=0, concat_axis=0, tiled=True)  30.8 us
    all_to_all x2, starting transfers between devices, exchange(): return lax.all_to_all(values, AXES, split_axis=0, concat_axis=0, tiled=True)  22.7 us
    pallas_call x1, Pallas kernels, add_quartets(): pl.pallas_call(quartet_kernel, out_shape=jax.ShapeDtypeStruct(blocks.shap...  12 us
    pallas_call x1, Pallas kernels, make_tables(): pl.pallas_call(table_kernel, grid=(classes,), out_shape=jax.ShapeDtypeStr...  6.38 us
    pallas_call x1, Pallas kernels, merge_blocks(): pl.pallas_call(merge_kernel, out_shape=jax.ShapeDtypeStruct(core.shape, j...  4.07 us
    pallas_call x1, Pallas kernels, pick_blocks(): pl.pallas_call(pick_kernel, out_shape=(jax.ShapeDtypeStruct((devices * SU...  3.15 us
    unnamed x18, local copies, waits for them, and re-layouts  2.68 us
  transfers between devices with their start and end apart: 2, of which 2 were waited for; matrix products, arithmetic and copies ran while one was open for 1% of the time, Pallas kernels for 7%

profile of v6, /device:TPU:1, one launch (start us, length us, event | category | flops | bytes accessed | tf_op | source)
XLA Modules:
  0.0 125.4 jit_solution(13672087635135988606)
XLA Ops:
  0.0 1.9 %ask_blocks.1 = s32[256,128]{1,0:T(8,128)} custom-call(s32[1,32]{1,0:T(1,128)} %work_ref.1, s32[5,128]{1,0:T(8,128)} %bitcast.27), custom_call_target="tpu_custom_call" | custom-call | tf_op jit(solution)/shard_map/ask_blocks/pallas_call | solution.py:71
  1.9 15.7 %all-to-all-start = ((s32[256,1,128]{2,1,0:T(1,128)}), s32[256,1,128]{2,1,0:T(1,128)S(1)}, u32[]{:S(2)}, u32[]{:S(2)}) async-start(s32[256,1,128]{2,1,0:T(1,128)} %bitcast.24), calls=%async_computation | async-start | bytes 262144 | tf_op jit(solution)/shard_map/all_to_all | solution.py:423
  17.6 0.0 copy-start
  17.6 1.4 %copy-done = f32[640,640]{1,0:T(8,128)S(1)} copy-done((f32[640,640]{1,0:T(8,128)S(1)}, f32[640,640]{1,0:T(8,128)}, u32[]{:S(2)}) %copy-start) | copy-done | bytes 1638424
  19.0 1.5 %flatten_blocks.1.flat_ref = f32[3200,128]{1,0:T(8,128)S(1)} custom-call(f32[640,640]{1,0:T(8,128)S(1)} %copy-done), custom_call_target="tpu_custom_call" | custom-call | tf_op jit(solution)/shard_map/flatten_blocks/pallas_call | solution.py:98
  20.5 10.1 %all-to-all-done = s32[256,1,128]{2,1,0:T(1,128)S(1)} async-done(((s32[256,1,128]{2,1,0:T(1,128)}), s32[256,1,128]{2,1,0:T(1,128)S(1)}, u32[]{:S(2)}, u32[]{:S(2)}) %all-to-all-start) | async-done | bytes 131104 | tf_op jit(solution)/shard_map/all_to_all | solution.py:423
  30.7 3.1 %pick_blocks.1 = (f32[2048,128]{1,0:T(8,128)}, s32[8,256]{1,0:T(8,128)S(1)}) custom-call(s32[256,128]{1,0:T(8,128)S(1)} %bitcast.23, f32[3200,128]{1,0:T(8,128)S(1)} %flatten_blocks.1.flat_ref), custom_call_target="tpu_custom_call" | custom-call | tf_op jit(solution)/shard_map/pick_blocks/pallas_call | solution.py:129
  33.8 0.0 copy-start.8
  33.8 7.1 %all-to-all-start.1 = ((f32[256,8,128]{2,1,0:T(8,128)}), f32[256,8,128]{2,1,0:T(8,128)}, u32[]{:S(2)}, u32[]{:S(2)}) async-start(f32[256,8,128]{2,1,0:T(8,128)} %bitcast.6), calls=%async_computation.1 | async-start | bytes 2097152 | tf_op jit(solution)/shard_map/all_to_all | solution.py:423
  41.5 0.0 copy-done.7
  41.5 0.1 reshape.74
  41.7 0.0 copy-done.8
  41.7 0.6 gather_fusion
  42.3 0.1 broadcast_in_dim.22
  42.4 0.1 broadcast_in_dim.23
  42.5 0.2 reshape.75.left_ref
  42.8 0.2 reshape.76.right_ref
  43.0 0.0 copy-start.2
  43.0 1.2 copy-done.2
  44.2 6.4 %make_tables.1.tables_ref = bf16[4,3,2,256,256]{4,3,2,1,0:T(8,128)(2,1)S(1)} custom-call(f32[4,256,256]{2,1,0:T(8,128)S(1)} %copy-done.2), custom_call_target="tpu_custom_call" | custom-call | tf_op jit(solution)/shard_map/make_tables/pallas_call | solution.py:249
  50.6 0.0 copy-done.3
  50.6 0.0 copy-done.4
  50.6 0.0 copy-done.5
  50.6 0.0 copy-done.6
  50.6 1.2 sort_quartets.1.rows_ref
  51.8 0.1 convert_reduce_fusion.ends_ref
  51.9 20.7 %all-to-all-done.1 = f32[256,8,128]{2,1,0:T(8,128)} async-done(((f32[256,8,128]{2,1,0:T(8,128)}), f32[256,8,128]{2,1,0:T(8,128)}, u32[]{:S(2)}, u32[]{:S(2)}) %all-to-all-start.1) | async-done | bytes 1048608 | tf_op jit(solution)/shard_map/all_to_all | solution.py:423
  72.7 12.0 %add_quartets.1 = f32[2048,128]{1,0:T(8,128)S(1)} custom-call(s32[4]{0:T(128)S(1)} %convert_reduce_fusion.ends_ref, f32[2048,128]{1,0:T(8,128)} %bitcast.7.blocks_ref, f32[16,8,128]{2,1,0:T(8,128)S(1)} %reshape.75.left_ref, f32[16,8,128]{2,1,0:T(8,128)S(1)} %reshape.76.right_ref, f32[8,512]{1,0:T(8,128)S(1)} %sort_quartets.1.rows_ref, ...), custom_call_target="tpu_custom_call" | custom-call | tf_op jit(solution)/shard_map/add_quartets/pallas_call | solution.py:404
  84.7 0.0 copy-start.1
  84.7 36.6 %all_to_all.15 = f32[256,8,128]{2,1,0:T(8,128)S(1)} all-to-all(f32[256,8,128]{2,1,0:T(8,128)S(1)} %bitcast.21), channel_id=1, replica_groups=mesh['row'=16,'col'=16] {'row','col'}, dimensions={0} | all-to-all | bytes 2097152 | tf_op jit(solution)/shard_map/all_to_all | solution.py:423
  121.3 0.0 copy-done.1
  121.4 4.1 %merge_blocks.1 = f32[640,640]{1,0:T(8,128)} custom-call(s32[8,256]{1,0:T(8,128)S(1)} %get-tuple-element.7.wanted_ref, f32[2048,128]{1,0:T(8,128)S(1)} %bitcast.22, f32[640,640]{1,0:T(8,128)S(1)} %copy-done.1), custom_call_target="tpu_custom_call" | custom-call | tf_op jit(solution)/shard_map/merge_blocks/pallas_call | solution.py:189
  (9 shorter events, 0.1 us)
Async XLA Ops:
  1.9 28.7 %all-to-all-start = ((s32[256,1,128]{2,1,0:T(1,128)}), s32[256,1,128]{2,1,0:T(1,128)S(1)}, u32[]{:S(2)}, u32[]{:S(2)}) async-start(s32[256,1,128]{2,1,0:T(1,128)} %bitcast.24), calls=%async_computation | async-start | bytes 262144 | tf_op jit(solution)/shard_map/all_to_all | solution.py:423
  17.6 1.4 %copy-start = (f32[640,640]{1,0:T(8,128)S(1)}, f32[640,640]{1,0:T(8,128)}, u32[]{:S(2)}) copy-start(f32[640,640]{1,0:T(8,128)} %density_ref.1) | copy-start | bytes 4915204
  30.6 10.9 %copy-start.7 = (f32[10240]{0:T(1024)S(1)}, f32[10240]{0:T(1024)}, u32[]{:S(2)}) copy-start(f32[10240]{0:T(1024)} %param.14) | copy-start | bytes 122884
  33.8 7.9 %copy-start.8 = (s32[1,32]{1,0:T(1,128)S(1)}, s32[1,32]{1,0:T(1,128)}, u32[]{:S(2)}) copy-start(s32[1,32]{1,0:T(1,128)} %work_ref.1) | copy-start | bytes 388
  33.8 38.9 %all-to-all-start.1 = ((f32[256,8,128]{2,1,0:T(8,128)}), f32[256,8,128]{2,1,0:T(8,128)}, u32[]{:S(2)}, u32[]{:S(2)}) async-start(f32[256,8,128]{2,1,0:T(8,128)} %bitcast.6), calls=%async_computation.1 | async-start | bytes 2097152 | tf_op jit(solution)/shard_map/all_to_all | solution.py:423
  43.0 1.2 copy-start.2
  44.2 6.4 %copy-start.3 = (s32[1,512]{1,0:T(1,128)S(1)}, s32[1,512]{1,0:T(1,128)}, u32[]{:S(2)}) copy-start(s32[1,512]{1,0:T(1,128)} %class_ref.1) | copy-start | bytes 6148
  44.2 6.4 %copy-start.4 = (s32[1,512]{1,0:T(1,128)S(1)}, s32[1,512]{1,0:T(1,128)}, u32[]{:S(2)}) copy-start(s32[1,512]{1,0:T(1,128)} %bra_ref.1) | copy-start | bytes 6148
  44.2 6.4 %copy-start.5 = (s32[1,512]{1,0:T(1,128)S(1)}, s32[1,512]{1,0:T(1,128)}, u32[]{:S(2)}) copy-start(s32[1,512]{1,0:T(1,128)} %ket_ref.1) | copy-start | bytes 6148
  44.2 6.4 %copy-start.6 = (f32[1,512]{1,0:T(1,128)S(1)}, f32[1,512]{1,0:T(1,128)}, u32[]{:S(2)}) copy-start(f32[1,512]{1,0:T(1,128)} %factor_ref.1) | copy-start | bytes 6148
  84.7 36.6 %copy-start.1 = (f32[640,640]{1,0:T(8,128)S(1)}, f32[640,640]{1,0:T(8,128)}, u32[]{:S(2)}) copy-start(f32[640,640]{1,0:T(8,128)} %core_ref.1) | copy-start | bytes 4915204
